TPU v7x, 512 devices: a whole 4x8x8 slice. The times are simulated.
512 devices in a mesh: section: 16 (over y, z_hi), inst: 4 (over x), tp: 8 (over z_lo, core).
Axes of the slice: x: 4, y: 8, z: 8 (z_hi: 2, z_lo: 4; z = z_hi * 4 + z_lo), core: 2. Of those that a mesh axis runs over, the one named last changes fastest.
Arguments:
- queries: bfloat16 [16, 128, 8192], P('section', 'inst', 'tp'), may hold values from -8 to 8
- new_kv: bfloat16 [16, 128, 2, 1024], P('section', 'inst', None, 'tp'), may hold values from -8 to 8
- kv_pages: bfloat16 [16, 512, 2, 64, 1024], P('section', 'inst', None, None, 'tp'), may hold values from -8 to 8
- lengths: int32 [16, 128], P('section'), may hold values from 1 to 448, as said below
- block_tables: int32 [16, 128, 7], P('section'), may hold values from 0 to 511, as said below
Outputs:
- attended: bfloat16 [16, 128, 8192], P('section', ('inst', 'tp'))
Inputs may be any that keep to these rules, and one draw needn't show every extreme that they name: `lengths`: some row of every layer has 448 tokens. `block_tables`: page p lies in the pool of instance p // 128. The pages that the rows of one layer use (positions k below ceil(lengths / 64)) are all different; entries at later positions are arbitrary page numbers.
All inputs are finite; a program needn't handle non-finite values.
Results may differ from a plain program's by a relative error of at most 0.0028.
Values may be sent and summed in bfloat16 or wider, within the bound.
A program may use at most 64 MiB of HBM per device.

v0:
```python
import math

import jax
import jax.numpy as jnp
from jax import lax
from jax.sharding import PartitionSpec as P

HEAD_DIM = 128
PAGE = 64
MAXP = 7


NEGATIVE = -1e30


def passed_along(block, axis, distance):
    devices = range(lax.axis_size(axis))
    route = [((i - distance) % len(devices), i) for i in devices]
    return lax.ppermute(block, axis, route)


def merge_sources(source_max, source_sum, source_out, head_size):
    highest = jnp.max(source_max, axis=1)
    factor = jnp.exp(source_max - highest[:, None])
    denominator = jnp.sum(source_sum * factor, axis=1)
    row_count, source_count, head_count = source_max.shape
    shaped = source_out.reshape(row_count, source_count, head_count, head_size)
    combined = jnp.sum(shaped * factor[..., None], axis=1)
    return (combined / denominator[..., None]).reshape(row_count, head_count * head_size)


def shards(queries, new_kv, kv_pages, lengths, block_tables):
    score_scale = 1.0 / math.sqrt(HEAD_DIM)
    home_rows = queries.shape[1]
    query_heads = queries.shape[2] // HEAD_DIM
    key_heads = new_kv.shape[3] // HEAD_DIM
    head_group = query_heads // key_heads
    pool_size = kv_pages.shape[1]
    all_rows = lengths.shape[1]
    instance = lax.axis_index("inst")
    gathered = lax.all_gather(queries[0], "inst", axis=0, tiled=True)
    layer_table = block_tables[0]
    layer_length = lengths[0]
    page_start = jnp.arange(MAXP, dtype=jnp.int32) * PAGE
    page_live = page_start[None, :] < layer_length[:, None]
    local_id = layer_table - instance * pool_size
    matched = (
        local_id[:, :, None] == jnp.arange(pool_size, dtype=jnp.int32)[None, None, :]
    ) & page_live[:, :, None]
    page_hits = matched.astype(jnp.int32)
    page_owner = jnp.sum(page_hits, axis=1)
    owner_row = jnp.sum(
        page_hits * jnp.arange(all_rows, dtype=jnp.int32)[:, None, None], axis=(0, 1)
    )
    page_slot = jnp.sum(page_hits * jnp.arange(MAXP, dtype=jnp.int32)[None, :, None], axis=(0, 1))
    page_used = jnp.sum(page_owner, axis=0) > 0
    page_query = jnp.take(gathered, owner_row, axis=0).reshape(
        pool_size, key_heads, head_group, HEAD_DIM
    )
    page_keys = kv_pages[0, :, 0].reshape(pool_size, PAGE, key_heads, HEAD_DIM)
    page_values = kv_pages[0, :, 1].reshape(pool_size, PAGE, key_heads, HEAD_DIM)
    scores = (
        jnp.einsum("phgd,pjhd->phgj", page_query, page_keys, preferred_element_type=jnp.float32)
        * score_scale
    )
    positions = page_slot[:, None] * PAGE + jnp.arange(PAGE, dtype=jnp.int32)[None, :]
    row_length = jnp.take(layer_length, owner_row)
    token_valid = (positions < row_length[:, None]) & page_used[:, None]
    token_mask = token_valid[:, None, None, :]
    scores = jnp.where(token_mask, scores, NEGATIVE)
    page_max = jnp.max(scores, axis=-1)
    weights = jnp.where(token_mask, jnp.exp(scores - page_max[..., None]), 0.0)
    page_sum = jnp.sum(weights, axis=-1)
    page_out = jnp.einsum(
        "phgj,pjhd->phgd",
        weights.astype(jnp.bfloat16),
        page_values,
        preferred_element_type=jnp.float32,
    )
    page_max = page_max.reshape(pool_size, query_heads)
    page_sum = page_sum.reshape(pool_size, query_heads)
    page_out = page_out.reshape(pool_size, query_heads, HEAD_DIM)
    owned = page_owner[:, :, None] > 0
    row_max = jnp.max(jnp.where(owned, page_max[None], NEGATIVE), axis=1)
    factor = jnp.exp(jnp.where(owned, page_max[None] - row_max[:, None], NEGATIVE))
    row_sum = jnp.sum(factor * page_sum[None], axis=1)
    row_out = jnp.einsum("rph,phd->rhd", factor, page_out, precision=lax.Precision.HIGHEST)
    own_query = queries[0].reshape(home_rows, key_heads, head_group, HEAD_DIM)
    own_key = new_kv[0, :, 0].reshape(home_rows, key_heads, HEAD_DIM)
    own_value = new_kv[0, :, 1].astype(jnp.float32).reshape(home_rows, key_heads, 1, HEAD_DIM)
    own_value = jnp.broadcast_to(own_value, (home_rows, key_heads, head_group, HEAD_DIM)).reshape(
        home_rows, query_heads, HEAD_DIM
    )
    own_score = (
        jnp.einsum("rhgd,rhd->rhg", own_query, own_key, preferred_element_type=jnp.float32)
        * score_scale
    )
    own_score = own_score.reshape(home_rows, query_heads)
    home_start = instance * home_rows
    home_max = lax.dynamic_slice_in_dim(row_max, home_start, home_rows, 0)
    home_sum = lax.dynamic_slice_in_dim(row_sum, home_start, home_rows, 0)
    home_out = lax.dynamic_slice_in_dim(row_out, home_start, home_rows, 0)
    highest = jnp.maximum(home_max, own_score)
    retain = jnp.exp(home_max - highest)
    own_weight = jnp.exp(own_score - highest)
    row_max = lax.dynamic_update_slice_in_dim(row_max, highest, home_start, 0)
    row_sum = lax.dynamic_update_slice_in_dim(
        row_sum, home_sum * retain + own_weight, home_start, 0
    )
    row_out = lax.dynamic_update_slice_in_dim(
        row_out, home_out * retain[..., None] + own_weight[..., None] * own_value, home_start, 0
    )
    stack_max = row_max[:, None, :]
    stack_sum = row_sum[:, None, :]
    stack_out = row_out.reshape(all_rows, 1, query_heads * HEAD_DIM)
    got_max, got_sum, got_out = (
        lax.all_to_all(stack_max, ("inst", "tp"), split_axis=0, concat_axis=1, tiled=True),
        lax.all_to_all(stack_sum, ("inst", "tp"), split_axis=0, concat_axis=1, tiled=True),
        lax.all_to_all(stack_out, ("inst", "tp"), split_axis=0, concat_axis=1, tiled=True),
    )
    part_rows = got_max.shape[0]
    instances = lax.axis_size("inst")
    head_width = got_max.shape[1] // instances * query_heads
    merged = merge_sources(
        got_max.reshape(part_rows, instances, head_width),
        got_sum.reshape(part_rows, instances, head_width),
        got_out.reshape(part_rows, instances, head_width * HEAD_DIM),
        HEAD_DIM,
    )
    result = passed_along(merged.astype(jnp.bfloat16), "section", 1)
    return result[None]


def solution(mesh):
    placed = (
        P("section", "inst", "tp"),
        P("section", "inst", None, "tp"),
        P("section", "inst", None, None, "tp"),
        P("section", None),
        P("section", None, None),
    )
    return jax.shard_map(
        shards,
        mesh=mesh,
        in_specs=placed,
        out_specs=P("section", ("inst", "tp"), None),
        check_vma=False,
    )
```

profile of v0, /device:TPU:1, one launch (start us, length us, event | category | flops | bytes accessed | tf_op | source)
XLA Modules:
  0.0 91.7 jit_solution(6478439472909798489)
XLA Ops:
  0.0 0.7 broadcast_subtract_fusion
  0.7 0.8 fusion.36
  1.5 0.7 broadcast_compare_fusion.1
  2.6 1.6 %gather_fusion = s32[128]{0:T(128)S(1)} fusion(s32[128]{0:T(128)} %bitcast.94, s32[1024]{0:T(1024)S(1)} %pad_clamp_fusion), kind=kCustom, calls=%fused_computation | custom fusion | bytes 1536 | tf_op jit(solution)/shard_map/jit(_take)/gather | solution.py:67
  4.2 10.8 %all-gather = bf16[1,128,1024]{2,1,0:T(8,128)(2,1)S(1)} all-gather(bf16[1,32,1024]{2,1,0:T(8,128)(2,1)} %param.5), channel_id=2, replica_groups=mesh['section'=16,'inst'=4,'tp'=8] {'inst'}, dimensions={1}, use_global_device_ids=true | all-gather | bytes 327680 | tf_op jit(solution)/shard_map/all_gather | solution.py:41
  15.0 0.9 copy.56
  16.1 0.9 gather_fusion.1
  17.3 2.9 %fusion.37 = (f32[128,8]{1,0:T(8,128)S(1)}, f32[128,8,64]{2,1,0:T(8,128)S(1)}) fusion(bf16[128,8,128]{2,1,0:T(8,128)(2,1)S(1)} %bitcast_select_fusion, bf16[1,128,2,64,128]{4,3,2,1,0:T(8,128)(2,1)} %param.7, pred[128,64]{1,0:T(8,128)(4,1)S(1)} %fusion.27), kind=kOutput, calls=%fused_computation.69 | convolution fusion | flops 16972800 | bytes 2633728 | tf_op jit(solution)/shard_map/phgd,pjhd->phgj/dot_general | solution.py:63
  20.3 0.4 fusion.16
  21.6 0.7 copy.47
  22.3 12.9 %all-to-all-start.2 = ((f32[128,1,8]{2,1,0:T(1,128)}), f32[128,1,8]{2,1,0:T(1,128)S(1)}, u32[]{:S(2)}, u32[]{:S(2)}) async-start(f32[128,1,8]{2,1,0:T(1,128)} %copy.47), calls=%async_computation.2 | async-start | bytes 131072 | tf_op jit(solution)/shard_map/all_to_all | solution.py:118
  35.3 2.3 %fusion = f32[128,8,128]{2,1,0:T(8,128)S(1)} fusion(bf16[1,128,2,64,128]{4,3,2,1,0:T(8,128)(2,1)} %param.7, f32[128,8,64]{2,1,0:T(8,128)S(1)} %get-tuple-element.18, f32[128,8]{1,0:T(8,128)S(1)} %get-tuple-element.17, pred[128,64]{1,0:T(8,128)(4,1)S(1)} %fusion.27), kind=kOutput, calls=%fused_computation.2 | convolution fusion | flops 16973824 | bytes 2895872 | tf_op jit(solution)/shard_map/phgj,pjhd->phgd/dot_general | solution.py:74
  37.6 1.3 %fusion.13 = f32[8,128,128]{2,1,0:T(8,128)S(1)} fusion(f32[128,8,128]{2,1,0:T(8,128)S(1)} %fusion, f32[128,8]{0,1:T(8,128)S(1)} %select_reduce_fusion, f32[128,8]{0,1:T(8,128)S(1)} %copy.38, pred[128,128]{1,0:T(8,128)(4,1)S(1)} %broadcast_compare_fusion), kind=kOutput, calls=%fused_computation.14 | convolution fusion | flops 201588736 | bytes 1073152 | tf_op jit(solution)/shard_map/rph,phd->rhd/dot_general | solution.py:87
  39.2 0.7 copy.44
  39.9 3.2 %all-to-all-done.2 = f32[128,1,8]{2,1,0:T(1,128)S(1)} async-done(((f32[128,1,8]{2,1,0:T(1,128)}), f32[128,1,8]{2,1,0:T(1,128)S(1)}, u32[]{:S(2)}, u32[]{:S(2)}) %all-to-all-start.2) | async-done | bytes 4128 | tf_op jit(solution)/shard_map/all_to_all | solution.py:118
  43.1 4.6 %all-to-all-start.1 = ((f32[128,1,8]{2,1,0:T(1,128)}), f32[128,1,8]{2,1,0:T(1,128)S(1)}, u32[]{:S(2)}, u32[]{:S(2)}) async-start(f32[128,1,8]{2,1,0:T(1,128)} %copy.44), calls=%async_computation.1 | async-start | bytes 131072 | tf_op jit(solution)/shard_map/all_to_all | solution.py:117
  47.9 1.1 %dynamic_update_slice.11 = f32[128,8,128]{0,2,1:T(8,128)S(1)} dynamic-update-slice(f32[128,8,128]{0,2,1:T(8,128)S(1)} %bitcast.96, f32[32,8,128]{0,2,1:T(8,128)S(1)} %fusion.12, s32[]{:T(128)S(6)} %select_n.68, s32[]{:T(128)} %constant.27.clone.1, s32[]{:T(128)} %constant.27.clone.1) | dynamic-update-slice | bytes 262148 | tf_op jit(solution)/shard_map/dynamic_update_slice | solution.py:110
  48.9 1.0 %copy.42 = f32[128,1,1024]{2,1,0:T(1,128)} copy(f32[128,1,1024]{0,2,1:T(8,128)S(1)} %bitcast.97) | data formatting | bytes 1048576 | tf_op jit(solution)/shard_map/reshape | solution.py:115
  50.0 5.5 %all-to-all-done.1 = f32[128,1,8]{2,1,0:T(1,128)S(1)} async-done(((f32[128,1,8]{2,1,0:T(1,128)}), f32[128,1,8]{2,1,0:T(1,128)S(1)}, u32[]{:S(2)}, u32[]{:S(2)}) %all-to-all-start.1) | async-done | bytes 4128 | tf_op jit(solution)/shard_map/all_to_all | solution.py:117
  55.4 4.0 %all-to-all-start = ((f32[128,1,1024]{2,1,0:T(1,128)}), f32[128,1,1024]{2,1,0:T(1,128)S(1)}, u32[]{:S(2)}, u32[]{:S(2)}) async-start(f32[128,1,1024]{2,1,0:T(1,128)} %copy.42), calls=%async_computation | async-start | bytes 1048576 | tf_op jit(solution)/shard_map/all_to_all | solution.py:119
  59.7 16.7 %all-to-all-done = f32[128,1,1024]{2,1,0:T(1,128)S(1)} async-done(((f32[128,1,1024]{2,1,0:T(1,128)}), f32[128,1,1024]{2,1,0:T(1,128)S(1)}, u32[]{:S(2)}, u32[]{:S(2)}) %all-to-all-start) | async-done | bytes 524320 | tf_op jit(solution)/shard_map/all_to_all | solution.py:119
  77.1 7.9 %collective-permute-start = (bf16[4,8192]{1,0:T(4,128)(2,1)S(1)}, bf16[4,8192]{1,0:T(4,128)(2,1)S(1)}, u32[]{:S(2)}, u32[]{:S(2)}) collective-permute-start(bf16[4,8192]{1,0:T(4,128)(2,1)S(1)} %bitcast.104), channel_id=1, source_target_pairs={{480,0},{0,32},{32,64},{64,96},{96,128},{128,160},{160,192},{192,2... | collective-permute-start | bytes 196616 | tf_op jit(solution)/shard_map/ppermute | solution.py:19
  85.1 6.0 %collective-permute-done = bf16[4,8192]{1,0:T(4,128)(2,1)S(1)} collective-permute-done((bf16[4,8192]{1,0:T(4,128)(2,1)S(1)}, bf16[4,8192]{1,0:T(4,128)(2,1)S(1)}, u32[]{:S(2)}, u32[]{:S(2)}) %collective-permute-start) | collective-permute-done | bytes 65568 | tf_op jit(solution)/shard_map/ppermute | solution.py:19
  91.1 0.6 copy.72
  (33 shorter events, 3.4 us)
Async XLA Ops:
  22.3 20.7 %all-to-all-start.2 = ((f32[128,1,8]{2,1,0:T(1,128)}), f32[128,1,8]{2,1,0:T(1,128)S(1)}, u32[]{:S(2)}, u32[]{:S(2)}) async-start(f32[128,1,8]{2,1,0:T(1,128)} %copy.47), calls=%async_computation.2 | async-start | bytes 131072 | tf_op jit(solution)/shard_map/all_to_all | solution.py:118
  43.1 12.4 %all-to-all-start.1 = ((f32[128,1,8]{2,1,0:T(1,128)}), f32[128,1,8]{2,1,0:T(1,128)S(1)}, u32[]{:S(2)}, u32[]{:S(2)}) async-start(f32[128,1,8]{2,1,0:T(1,128)} %copy.44), calls=%async_computation.1 | async-start | bytes 131072 | tf_op jit(solution)/shard_map/all_to_all | solution.py:117
  55.4 20.9 %all-to-all-start = ((f32[128,1,1024]{2,1,0:T(1,128)}), f32[128,1,1024]{2,1,0:T(1,128)S(1)}, u32[]{:S(2)}, u32[]{:S(2)}) async-start(f32[128,1,1024]{2,1,0:T(1,128)} %copy.42), calls=%async_computation | async-start | bytes 1048576 | tf_op jit(solution)/shard_map/all_to_all | solution.py:119
  77.1 13.9 %collective-permute-start = (bf16[4,8192]{1,0:T(4,128)(2,1)S(1)}, bf16[4,8192]{1,0:T(4,128)(2,1)S(1)}, u32[]{:S(2)}, u32[]{:S(2)}) collective-permute-start(bf16[4,8192]{1,0:T(4,128)(2,1)S(1)} %bitcast.104), channel_id=1, source_target_pairs={{480,0},{0,32},{32,64},{64,96},{96,128},{128,160},{160,192},{192,2... | collective-permute-start | bytes 196616 | tf_op jit(solution)/shard_map/ppermute | solution.py:19
where the time goes:
time: 92.3 us; the launch traced here: 91.7 us
  waiting for transfers between devices  31.3 us (34%)
  starting transfers between devices  29.5 us (32%)
  blocking collectives  10.8 us (12%)
  local copies, waits for them, and re-layouts  8.8 us (10%)
  matrix products  6.62 us (7%)
  other arithmetic  4.57 us (5%)
    all_to_all x1, waiting for transfers between devices, shards(): lax.all_to_all(stack_out, ('inst', 'tp'), split_axis=0, concat_axis=1, ti...  16.7 us
    all_to_all x1, starting transfers between devices, shards(): lax.all_to_all(stack_sum, ('inst', 'tp'), split_axis=0, concat_axis=1, ti...  12.9 us
    all_gather x1, blocking collectives, shards(): gathered = lax.all_gather(queries[0], 'inst', axis=0, tiled=True)  10.8 us
    ppermute x1, starting transfers between devices, passed_along(): return lax.ppermute(block, axis, route)  7.94 us
    ppermute x1, waiting for transfers between devices, passed_along(): return lax.ppermute(block, axis, route)  5.99 us
    all_to_all x1, waiting for transfers between devices, shards(): lax.all_to_all(stack_max, ('inst', 'tp'), split_axis=0, concat_axis=1, ti...  5.46 us
    all_to_all x1, starting transfers between devices, shards(): lax.all_to_all(stack_max, ('inst', 'tp'), split_axis=0, concat_axis=1, ti...  4.59 us
    all_to_all x1, starting transfers between devices, shards(): lax.all_to_all(stack_out, ('inst', 'tp'), split_axis=0, concat_axis=1, ti...  4 us
  transfers between devices with their start and end apart: 4, of which 4 were waited for; matrix products, arithmetic and copies ran while one was open for 8% of the time, Pallas kernels for 0%

commit v1 on v0

v1 whole, which is shorter than its diff:
```python
import functools
import math

import jax
import jax.numpy as jnp
from jax import lax
from jax.experimental import pallas as pl
from jax.experimental.pallas import tpu as pltpu
from jax.sharding import PartitionSpec as P

HEAD_DIM = 128
NEGATIVE = -1e30
GROUP = 8
MESH = pl.DeviceIdType.MESH
F32 = jnp.float32
BF16 = jnp.bfloat16


def iota(shape, dim):
    return lax.broadcasted_iota(jnp.int32, shape, dim)


def dot(a, b):
    return lax.dot_general(a, b, (((1,), (0,)), ((), ())), preferred_element_type=F32)


def dot_nt(a, b):
    return lax.dot_general(a, b, (((1,), (1,)), ((), ())), preferred_element_type=F32)


def split(x):
    high = x.astype(BF16)
    return high, (x - high.astype(F32)).astype(BF16)


def kernel(
    sizes,
    q_hbm,
    fresh_hbm,
    kv_hbm,
    len_hbm,
    table_hbm,
    out_ref,
    q_all,
    fresh,
    fresh_f,
    kv,
    length,
    table,
    page_x,
    page_m,
    page_s,
    p_send,
    p_recv,
    r_send,
    load_sem,
    kv_sem,
    q_ssem,
    q_rsem,
    p_ssem,
    p_rsem,
    r_ssem,
    r_rsem,
):
    sections, insts, tps, home, pool, slots, page, heads = sizes
    rows = home * insts
    part = home // tps
    scale = 1.0 / math.sqrt(HEAD_DIM)
    sec = lax.axis_index("section")
    me = lax.axis_index("inst")
    tp = lax.axis_index("tp")
    my_rows = pl.ds(pl.multiple_of(me * home, home), home)

    load_q = pltpu.make_async_copy(q_hbm, q_all.at[my_rows], load_sem.at[0])
    load_fresh = pltpu.make_async_copy(fresh_hbm, fresh, load_sem.at[1])
    load_len = pltpu.make_async_copy(len_hbm, length, load_sem.at[2])
    load_table = pltpu.make_async_copy(table_hbm, table, load_sem.at[3])
    load_q.start()
    load_table.start()
    load_len.start()
    load_fresh.start()

    barrier = pltpu.get_barrier_semaphore()
    for o in range(1, insts):
        pl.semaphore_signal(
            barrier, inc=1, device_id={"inst": lax.rem(me + o, insts)}, device_id_type=MESH
        )
    before = lax.rem(sec + sections - 1, sections)
    after = lax.rem(sec + 1, sections)
    for t in range(tps):
        pl.semaphore_signal(
            barrier, inc=1, device_id={"section": before, "tp": t}, device_id_type=MESH
        )
    chunks = kv_sem.shape[0]
    per = pool // chunks
    load_kv = [
        pltpu.make_async_copy(
            kv_hbm.at[pl.ds(c * per, per)], kv.at[pl.ds(c * per, per)], kv_sem.at[c]
        )
        for c in range(chunks)
    ]
    for copy in load_kv:
        copy.start()

    load_q.wait()
    pl.semaphore_wait(barrier, insts - 1 + tps)

    q_copies = []
    for o in (2, 1, 3):
        copy = pltpu.make_async_remote_copy(
            src_ref=q_all.at[my_rows],
            dst_ref=q_all.at[my_rows],
            send_sem=q_ssem.at[o - 1],
            recv_sem=q_rsem.at[o - 1],
            device_id={"inst": lax.rem(me + o, insts)},
            device_id_type=MESH,
        )
        copy.start()
        q_copies.append(copy)

    load_len.wait()
    load_table.wait()
    page_id = iota((pool, rows), 0)
    counted = jnp.zeros((pool, rows), jnp.int32)
    for k in range(slots):
        local = table[k] - me * pool
        live = jnp.clip(length[...] - k * page, 0, page)
        counted = counted + jnp.where(page_id == local, live, 0)
    owned = counted > 0
    owner_f = jnp.where(owned, 1.0, 0.0).astype(F32)
    owner = owner_f.astype(BF16)
    owner_t = owner_f.T.astype(BF16)
    owner_t2 = jnp.concatenate([owner_t, owner_t], axis=1)
    tokens = dot(counted.astype(F32).astype(BF16), jnp.ones((rows, 128), BF16))

    load_fresh.wait()
    fresh_f[...] = fresh[...].astype(F32)
    own_k = fresh_f[pl.ds(0, home, stride=2), :]
    own_v = fresh_f[pl.ds(1, home, stride=2), :]
    lane = iota((home, 128), 1)
    own = jnp.zeros((home, 128), F32)
    q_mine = q_all[my_rows, :].astype(F32)
    for h in range(heads):
        score = jnp.sum(q_mine[:, h * 128 : (h + 1) * 128] * own_k, axis=1, keepdims=True) * scale
        own = jnp.where(lane == h, score, own)

    for copy in q_copies:
        copy.wait_recv()
    picked = dot(owner, q_all[...])
    for copy in load_kv:
        copy.wait()

    stack = heads * GROUP
    row_page = lax.rem(iota((stack, 128), 0), GROUP)
    per_tile = 128 // page
    tiles = GROUP // per_tile
    tile_of = row_page // per_tile
    token = iota((stack, 128), 1) - lax.rem(row_page, per_tile) * page
    token_f = token.astype(F32)
    for g in range(pool // GROUP):
        at = slice(g * GROUP, (g + 1) * GROUP)
        group_q = jnp.concatenate(
            [picked[at, h * 128 : (h + 1) * 128] for h in range(heads)], axis=0
        ).astype(BF16)
        keys = kv[at, 0].reshape(GROUP * page, 128)
        values = kv[at, 1].reshape(GROUP * page, 128)
        full = dot_nt(group_q, keys)
        scores = full[:, :128]
        for c in range(1, tiles):
            scores = jnp.where(tile_of == c, full[:, c * 128 : (c + 1) * 128], scores)
        limit = jnp.concatenate([tokens[at]] * heads, axis=0)
        valid = (token >= 0) & (token_f < limit)
        scores = jnp.where(valid, scores * scale, NEGATIVE)
        highest = jnp.max(scores, axis=1, keepdims=True)
        weights = jnp.where(valid, jnp.exp(scores - highest), 0.0)
        total = jnp.sum(weights, axis=1, keepdims=True)
        spread = jnp.concatenate(
            [jnp.where(tile_of == c, weights, 0.0).astype(BF16) for c in range(tiles)], axis=1
        )
        x = dot(spread, values)
        page_x[:, at, :] = x.reshape(heads, GROUP, 128)
        page_m[:, at, :] = jnp.broadcast_to(highest, (stack, 128)).reshape(heads, GROUP, 128)
        page_s[:, at, :] = jnp.broadcast_to(total, (stack, 128)).reshape(heads, GROUP, 128)

    refs = []
    for h in range(heads):
        rounded = page_m[h].astype(BF16).astype(F32)
        refs.append(jnp.max(jnp.where(owned, rounded, NEGATIVE), axis=0, keepdims=True))
    sums = jnp.zeros((pool, 128), F32)
    pool_lane = iota((pool, 128), 1)
    for h in range(0, heads, 2):
        sides = []
        for j in (h, h + 1):
            page_ref = dot_nt(owner, jnp.broadcast_to(refs[j], (128, rows)).astype(BF16))
            factor = jnp.exp(page_m[j] - page_ref)
            sums = jnp.where(pool_lane == heads + j, factor * page_s[j], sums)
            high, low = split(factor * page_x[j])
            sides.append(jnp.concatenate([high, low], axis=0))
        both = dot(owner_t2, jnp.concatenate(sides, axis=1))
        for d in range(insts):
            for j in range(2):
                p_send[d, (h + j) * home : (h + j + 1) * home, :] = both[
                    d * home : (d + 1) * home, j * 128 : (j + 1) * 128
                ]
    high, low = split(sums)
    stat = dot(owner_t2, jnp.concatenate([high, low], axis=0))
    ref_pad = jnp.concatenate(refs + [jnp.zeros((128 - heads, rows), F32)], axis=0)
    stat = stat + ref_pad.T
    for d in range(insts):
        p_send[d, heads * home :, :] = stat[d * home : (d + 1) * home]

    p_copies = []
    for o in (2, 1, 3):
        to = lax.rem(me + o, insts)
        copy = pltpu.make_async_remote_copy(
            src_ref=p_send.at[to],
            dst_ref=p_recv.at[o - 1],
            send_sem=p_ssem.at[o - 1],
            recv_sem=p_rsem.at[o - 1],
            device_id={"inst": to},
            device_id_type=MESH,
        )
        copy.start()
        p_copies.append(copy)
    for copy in p_copies:
        copy.wait_recv()

    stats = [p_send[me, heads * home :, :]]
    stats += [p_recv[o, heads * home :, :] for o in range(insts - 1)]
    highest = own
    for s in stats:
        highest = jnp.maximum(highest, s)
    own_factor = jnp.exp(own - highest)
    total = own_factor
    factors = []
    for s in stats:
        f = jnp.exp(s - highest)
        total = total + f * pltpu.roll(s, 128 - heads, 1)
        factors.append(f)
    inverse = 1.0 / total
    own_factor = own_factor * inverse
    factors = [f * inverse for f in factors]
    merged = []
    for h in range(heads):
        at = slice(h * home, (h + 1) * home)
        acc = own_factor[:, h : h + 1] * own_v
        acc = acc + factors[0][:, h : h + 1] * p_send[me, at, :]
        for o in range(insts - 1):
            acc = acc + factors[o + 1][:, h : h + 1] * p_recv[o, at, :]
        merged.append(acc)

    lower = iota((8, 128), 0) < part
    for u in range(home // 8):
        first, second = [], []
        for h in range(0, heads, 2):
            a = merged[h][u * 8 : (u + 1) * 8]
            b = merged[h + 1][u * 8 : (u + 1) * 8]
            first.append(jnp.where(lower, a, pltpu.roll(b, part, 0)))
            second.append(jnp.where(lower, pltpu.roll(a, part, 0), b))
        r_send[2 * u] = jnp.concatenate(first, axis=0).astype(BF16)
        r_send[2 * u + 1] = jnp.concatenate(second, axis=0).astype(BF16)
    r_copies = []
    for t in range(tps):
        copy = pltpu.make_async_remote_copy(
            src_ref=r_send.at[t],
            dst_ref=out_ref.at[tp],
            send_sem=r_ssem.at[t],
            recv_sem=r_rsem.at[tp],
            device_id={"section": after, "tp": t},
            device_id_type=MESH,
        )
        copy.start()
        r_copies.append(copy)
    for t in range(tps):
        pltpu.make_async_remote_copy(
            src_ref=r_send.at[t],
            dst_ref=out_ref.at[t],
            send_sem=r_ssem.at[t],
            recv_sem=r_rsem.at[t],
            device_id={"section": after, "tp": t},
            device_id_type=MESH,
        ).wait_recv()
    for copy in q_copies + p_copies + r_copies:
        copy.wait_send()


def shards(queries, new_kv, kv_pages, lengths, block_tables):
    sections = lax.axis_size("section")
    insts = lax.axis_size("inst")
    tps = lax.axis_size("tp")
    home = queries.shape[1]
    heads = queries.shape[2] // HEAD_DIM
    pool, page = kv_pages.shape[1], kv_pages.shape[3]
    rows, slots = block_tables.shape[1:]
    part = home // tps
    sizes = (sections, insts, tps, home, pool, slots, page, heads)
    message = (heads + 1) * home
    out = pl.pallas_call(
        functools.partial(kernel, sizes),
        out_shape=jax.ShapeDtypeStruct((tps, heads * part, HEAD_DIM), BF16),
        in_specs=[pl.BlockSpec(memory_space=pl.ANY)] * 5,
        out_specs=pl.BlockSpec(memory_space=pl.ANY),
        scratch_shapes=[
            pltpu.VMEM((rows, heads * HEAD_DIM), BF16),
            pltpu.VMEM((2 * home, HEAD_DIM), BF16),
            pltpu.VMEM((2 * home, HEAD_DIM), F32),
            pltpu.VMEM((pool, 2, page, HEAD_DIM), BF16),
            pltpu.VMEM((1, rows), jnp.int32),
            pltpu.VMEM((slots, 1, rows), jnp.int32),
            pltpu.VMEM((heads, pool, HEAD_DIM), F32),
            pltpu.VMEM((heads, pool, HEAD_DIM), F32),
            pltpu.VMEM((heads, pool, HEAD_DIM), F32),
            pltpu.VMEM((insts, message, HEAD_DIM), F32),
            pltpu.VMEM((insts - 1, message, HEAD_DIM), F32),
            pltpu.VMEM((tps, heads * part, HEAD_DIM), BF16),
            pltpu.SemaphoreType.DMA((4,)),
            pltpu.SemaphoreType.DMA((4,)),
            pltpu.SemaphoreType.DMA((insts - 1,)),
            pltpu.SemaphoreType.DMA((insts - 1,)),
            pltpu.SemaphoreType.DMA((insts - 1,)),
            pltpu.SemaphoreType.DMA((insts - 1,)),
            pltpu.SemaphoreType.DMA((tps,)),
            pltpu.SemaphoreType.DMA((tps,)),
        ],
        compiler_params=pltpu.CompilerParams(
            collective_id=0, has_side_effects=True, vmem_limit_bytes=32 * 1024 * 1024
        ),
    )(
        queries[0],
        new_kv[0].reshape(2 * home, HEAD_DIM),
        kv_pages[0],
        lengths,
        block_tables[0].T.reshape(slots, 1, rows),
    )
    out = out.reshape(tps, heads, part, HEAD_DIM).transpose(2, 0, 1, 3)
    return out.reshape(1, part, tps * heads * HEAD_DIM)


def solution(mesh):
    placed = (
        P("section", "inst", "tp"),
        P("section", "inst", None, "tp"),
        P("section", "inst", None, None, "tp"),
        P("section", None),
        P("section", None, None),
    )
    return jax.shard_map(
        shards,
        mesh=mesh,
        in_specs=placed,
        out_specs=P("section", ("inst", "tp"), None),
        check_vma=False,
    )
```

time: 92.3 us -> 43.1 us (0.47)
  Pallas kernels: 0 us -> 37.1 us
  waiting for transfers between devices: 31.3 us -> 0 us
  starting transfers between devices: 29.5 us -> 0 us
  blocking collectives: 10.8 us -> 0 us
  matrix products: 6.62 us -> 0 us
  other arithmetic: 4.57 us -> 0 us
  local copies, waits for them, and re-layouts: 8.8 us -> 5.72 us
    pallas_call x0 -> x1, Pallas kernels: none -> 37.1 us  [shards(): pl.pallas_call(functools.partial(kernel, sizes), out_shape=jax.ShapeDtype...]
    all_to_all x3 -> x0, waiting for transfers between devices: 25.3 us -> none  [the longest x1 16.7 us: shards(): lax.all_to_all(stack_out, ('inst', 'tp'), split_axis=0, concat_axis=1, ti...]
    all_to_all x3 -> x0, starting transfers between devices: 21.5 us -> none  [the longest x1 12.9 us: shards(): lax.all_to_all(stack_sum, ('inst', 'tp'), split_axis=0, concat_axis=1, ti...]
    all_gather x1 -> x0, blocking collectives: 10.8 us -> none  [shards(): gathered = lax.all_gather(queries[0], 'inst', axis=0, tiled=True)]
    ppermute x1 -> x0, starting transfers between devices: 7.94 us -> none  [passed_along(): return lax.ppermute(block, axis, route)]
    dot_general x4 -> x0, matrix products: 6.62 us -> none  [the longest x1 2.89 us: shards(): jnp.einsum('phgd,pjhd->phgj', page_query, page_keys, preferred_element_ty...]
    ppermute x1 -> x0, waiting for transfers between devices: 5.99 us -> none  [passed_along(): return lax.ppermute(block, axis, route)]
    unnamed x6 -> x10, local copies, waits for them, and re-layouts: 1.59 us -> 5.72 us
  transfers between devices with their start and end apart: 4 -> 0, of which waited for: 4 -> 0; matrix products, arithmetic and copies ran while one was open for 8% -> 0% of each run, Pallas kernels for 0% -> 0%
where the time goes in v1:
time: 43.1 us; the launch traced here: 42.9 us
  Pallas kernels  37.1 us (86%)
  local copies, waits for them, and re-layouts  5.72 us (13%)
    pallas_call x1, Pallas kernels, shards(): pl.pallas_call(functools.partial(kernel, sizes), out_shape=jax.ShapeDtype...  37.1 us
    unnamed x10, local copies, waits for them, and re-layouts  5.72 us

profile of v1, /device:TPU:1, one launch (start us, length us, event | category | flops | bytes accessed | tf_op | source)
XLA Modules:
  0.0 42.9 jit_solution(2857136641426925047)
XLA Ops:
  0.0 0.7 %copy.9 = s32[1,128,7]{1,2,0:T(8,128)S(1)} copy(s32[1,128,7]{1,0,2:T(1,128)} %param.9) | data formatting | bytes 7168
  0.7 0.0 copy-start
  0.7 2.2 %copy-done = bf16[1,128,2,64,128]{4,3,2,1,0:T(8,128)(2,1)S(1)} copy-done((bf16[1,128,2,64,128]{4,3,2,1,0:T(8,128)(2,1)S(1)}, bf16[1,128,2,64,128]{4,3,2,1,0:T(8,128)(2,1)}, u32[]{:S(2)}) %copy-start) | copy-done | bytes 4194328
  2.9 0.0 copy-start.1
  2.9 0.8 %copy-done.1 = bf16[1,32,1024]{2,1,0:T(8,128)(2,1)S(1)} copy-done((bf16[1,32,1024]{2,1,0:T(8,128)(2,1)S(1)}, bf16[1,32,1024]{2,1,0:T(8,128)(2,1)}, u32[]{:S(2)}) %copy-start.1) | copy-done | bytes 65560
  3.7 0.0 copy-start.2
  3.7 0.7 %copy-done.2 = bf16[1,32,2,128]{3,2,1,0:T(2,128)(2,1)S(1)} copy-done((bf16[1,32,2,128]{3,2,1,0:T(2,128)(2,1)S(1)}, bf16[1,32,2,128]{3,2,1,0:T(2,128)(2,1)}, u32[]{:S(2)}) %copy-start.2) | copy-done | bytes 16408
  4.4 0.0 copy-start.3
  4.4 0.7 %copy-done.3 = s32[1,128]{1,0:T(1,128)S(1)} copy-done((s32[1,128]{1,0:T(1,128)S(1)}, s32[1,128]{1,0:T(1,128)}, u32[]{:S(2)}) %copy-start.3) | copy-done | bytes 536
  5.1 37.1 %shard_map.55 = bf16[8,32,128]{2,1,0:T(8,128)(2,1)S(1)} custom-call(bf16[32,1024]{1,0:T(8,128)(2,1)S(1)} %bitcast.15, bf16[64,128]{1,0:T(8,128)(2,1)S(1)} %bitcast.16, bf16[128,2,64,128]{3,2,1,0:T(8,128)(2,1)S(1)} %bitcast.13, s32[1,128]{1,0:T(1,128)S(1)} %copy-done.3, s32[7,1,128]{2,1,0:T(1,128)S(1)} %reshape.9.table_hbm), custom_call_target="tpu_custom_call" | custom-call | tf_op jit(solution)/shard_map/pallas_call | solution.py:298
  42.2 0.6 %copy.11 = bf16[1,4,8192]{2,1,0:T(4,128)(2,1)} copy(bf16[1,4,8192]{2,1,0:T(4,128)(2,1)S(1)} %bitcast.14) | data formatting | bytes 131072
  (1 shorter events, 0.0 us)
Async XLA Ops:
  0.7 2.2 %copy-start = (bf16[1,128,2,64,128]{4,3,2,1,0:T(8,128)(2,1)S(1)}, bf16[1,128,2,64,128]{4,3,2,1,0:T(8,128)(2,1)}, u32[]{:S(2)}) copy-start(bf16[1,128,2,64,128]{4,3,2,1,0:T(8,128)(2,1)} %param.7) | copy-start | bytes 12582916
  2.9 0.8 %copy-start.1 = (bf16[1,32,1024]{2,1,0:T(8,128)(2,1)S(1)}, bf16[1,32,1024]{2,1,0:T(8,128)(2,1)}, u32[]{:S(2)}) copy-start(bf16[1,32,1024]{2,1,0:T(8,128)(2,1)} %param.5) | copy-start | bytes 196612
  3.7 0.7 %copy-start.2 = (bf16[1,32,2,128]{3,2,1,0:T(2,128)(2,1)S(1)}, bf16[1,32,2,128]{3,2,1,0:T(2,128)(2,1)}, u32[]{:S(2)}) copy-start(bf16[1,32,2,128]{3,2,1,0:T(2,128)(2,1)} %param.6) | copy-start | bytes 49156
  4.4 0.7 %copy-start.3 = (s32[1,128]{1,0:T(1,128)S(1)}, s32[1,128]{1,0:T(1,128)}, u32[]{:S(2)}) copy-start(s32[1,128]{1,0:T(1,128)} %len_hbm.1) | copy-start | bytes 1540

commit v2 on v1

v2 whole, which is shorter than its diff:
```python
import functools
import math

import jax
import jax.numpy as jnp
from jax import lax
from jax.experimental import pallas as pl
from jax.experimental.pallas import tpu as pltpu
from jax.sharding import PartitionSpec as P

HEAD_DIM = 128
NEGATIVE = -1e30
GROUP = 8
CHUNKS = 2
ORDER = (2, 1, 3)
LEVELS = 32767.0
TINY = 1e-30
MESH = pl.DeviceIdType.MESH
F32 = jnp.float32
BF16 = jnp.bfloat16


def iota(shape, dim):
    return lax.broadcasted_iota(jnp.int32, shape, dim)


def dot(a, b):
    return lax.dot_general(a, b, (((1,), (0,)), ((), ())), preferred_element_type=F32)


def dot_nt(a, b):
    return lax.dot_general(a, b, (((1,), (1,)), ((), ())), preferred_element_type=F32)


def split(x):
    high = x.astype(BF16)
    return high, (x - high.astype(F32)).astype(BF16)


def kernel(
    sizes,
    q_hbm,
    fresh_hbm,
    kv_hbm,
    len_hbm,
    table_hbm,
    out_ref,
    q_all,
    fresh,
    fresh_f,
    kv,
    length,
    table,
    score_buf,
    weight_buf,
    page_x,
    page_m,
    page_s,
    p_send,
    p_recv,
    s_send,
    s_recv,
    r_send,
    load_sem,
    kv_sem,
    q_ssem,
    q_rsem,
    p_ssem,
    p_rsem,
    s_ssem,
    s_rsem,
    r_ssem,
    r_rsem,
):
    sections, insts, tps, home, pool, slots, page, heads = sizes
    rows = home * insts
    part = home // tps
    scale = 1.0 / math.sqrt(HEAD_DIM)
    sec = lax.axis_index("section")
    me = lax.axis_index("inst")
    tp = lax.axis_index("tp")
    before = lax.rem(sec + sections - 1, sections)
    after = lax.rem(sec + 1, sections)
    my_rows = pl.ds(pl.multiple_of(me * home, home), home)

    barrier = pltpu.get_barrier_semaphore()
    for o in range(1, insts):
        pl.semaphore_signal(
            barrier, inc=1, device_id={"inst": lax.rem(me + o, insts)}, device_id_type=MESH
        )
    for t in range(tps):
        pl.semaphore_signal(
            barrier, inc=1, device_id={"section": before, "tp": t}, device_id_type=MESH
        )
    load_q = pltpu.make_async_copy(q_hbm, q_all.at[my_rows], load_sem.at[0])
    load_fresh = pltpu.make_async_copy(fresh_hbm, fresh, load_sem.at[1])
    load_len = pltpu.make_async_copy(len_hbm, length, load_sem.at[2])
    load_table = pltpu.make_async_copy(table_hbm, table, load_sem.at[3])
    load_table.start()
    load_len.start()
    pl.semaphore_wait(barrier, insts - 1 + tps)

    q_copies = []
    for o in ORDER:
        copy = pltpu.make_async_remote_copy(
            src_ref=q_hbm,
            dst_ref=q_all.at[my_rows],
            send_sem=q_ssem.at[o - 1],
            recv_sem=q_rsem.at[o - 1],
            device_id={"inst": lax.rem(me + o, insts)},
            device_id_type=MESH,
        )
        copy.start()
        q_copies.append(copy)
    load_q.start()
    load_fresh.start()
    chunks = kv_sem.shape[0]
    per = pool // chunks
    load_kv = [
        pltpu.make_async_copy(
            kv_hbm.at[pl.ds(c * per, per)], kv.at[pl.ds(c * per, per)], kv_sem.at[c]
        )
        for c in range(chunks)
    ]
    for copy in load_kv:
        copy.start()

    load_len.wait()
    load_table.wait()
    page_id = iota((pool, rows), 0)
    counted = jnp.zeros((pool, rows), jnp.int32)
    for k in range(slots):
        local = table[k] - me * pool
        live = jnp.clip(length[...] - k * page, 0, page)
        counted = counted + jnp.where(page_id == local, live, 0)
    owned = counted > 0
    owner_f = jnp.where(owned, 1.0, 0.0).astype(F32)
    owner = owner_f.astype(BF16)
    owner_t = owner_f.T.astype(BF16)
    owner_t2 = jnp.concatenate([owner_t, owner_t], axis=1)
    tokens = dot(counted.astype(F32).astype(BF16), jnp.ones((rows, 128), BF16))

    load_fresh.wait()
    load_q.wait()
    fresh_f[...] = fresh[...].astype(F32)
    own_k = fresh_f[pl.ds(0, home, stride=2), :]
    own_v = fresh_f[pl.ds(1, home, stride=2), :]
    lane = iota((home, 128), 1)
    own = jnp.zeros((home, 128), F32)
    q_mine = q_all[my_rows, :].astype(F32)
    for h in range(heads):
        score = jnp.sum(q_mine[:, h * 128 : (h + 1) * 128] * own_k, axis=1, keepdims=True) * scale
        own = jnp.where(lane == h, score, own)

    for copy in load_kv:
        copy.wait()
    for copy in q_copies:
        copy.wait_recv()
    picked = dot(owner, q_all[...])

    stack = heads * GROUP
    groups = pool // GROUP
    row_page = lax.rem(iota((stack, 128), 0), GROUP)
    per_tile = 128 // page
    tiles = GROUP // per_tile
    tile_of = row_page // per_tile
    token = iota((stack, 128), 1) - lax.rem(row_page, per_tile) * page
    token_f = token.astype(F32)
    for g in range(groups):
        at = slice(g * GROUP, (g + 1) * GROUP)
        group_q = jnp.concatenate(
            [picked[at, h * 128 : (h + 1) * 128] for h in range(heads)], axis=0
        ).astype(BF16)
        full = dot_nt(group_q, kv[at, 0].reshape(GROUP * page, 128))
        scores = full[:, :128]
        for c in range(1, tiles):
            scores = jnp.where(tile_of == c, full[:, c * 128 : (c + 1) * 128], scores)
        score_buf[g] = scores
    for g in range(groups):
        at = slice(g * GROUP, (g + 1) * GROUP)
        limit = jnp.concatenate([tokens[at]] * heads, axis=0)
        valid = (token >= 0) & (token_f < limit)
        scores = jnp.where(valid, score_buf[g] * scale, NEGATIVE)
        highest = jnp.max(scores, axis=1, keepdims=True)
        weights = jnp.where(valid, jnp.exp(scores - highest), 0.0)
        total = jnp.sum(weights, axis=1, keepdims=True)
        weight_buf[g] = weights
        page_m[:, at, :] = jnp.broadcast_to(highest, (stack, 128)).reshape(heads, GROUP, 128)
        page_s[:, at, :] = jnp.broadcast_to(total, (stack, 128)).reshape(heads, GROUP, 128)
    for g in range(groups):
        at = slice(g * GROUP, (g + 1) * GROUP)
        weights = weight_buf[g]
        spread = jnp.concatenate(
            [jnp.where(tile_of == c, weights, 0.0).astype(BF16) for c in range(tiles)], axis=1
        )
        x = dot(spread, kv[at, 1].reshape(GROUP * page, 128))
        page_x[:, at, :] = x.reshape(heads, GROUP, 128)

    refs = []
    for h in range(heads):
        rounded = page_m[h].astype(BF16).astype(F32)
        refs.append(jnp.max(jnp.where(owned, rounded, NEGATIVE), axis=0, keepdims=True))
    ref_t = jnp.concatenate(refs + [jnp.zeros((128 - heads, rows), F32)], axis=0).T
    pool_lane = iota((pool, 128), 1)
    row_lane = iota((rows, 128), 1)
    span = heads // CHUNKS
    wide = span * home
    p_copies, s_copies = [], []
    for c in range(CHUNKS):
        chunk = range(c * span, (c + 1) * span)
        sums = jnp.zeros((pool, 128), F32)
        stat = jnp.where(row_lane < heads, ref_t, 0.0)
        for h in chunk[::2]:
            sides = []
            for j in (h, h + 1):
                page_ref = dot_nt(owner, jnp.broadcast_to(refs[j], (128, rows)).astype(BF16))
                factor = jnp.exp(page_m[j] - page_ref)
                sums = jnp.where(pool_lane == heads + j, factor * page_s[j], sums)
                high, low = split(factor * page_x[j])
                sides.append(jnp.concatenate([high, low], axis=0))
            both = dot(owner_t2, jnp.concatenate(sides, axis=1))
            for j in range(2):
                x = both[:, j * 128 : (j + 1) * 128]
                largest = jnp.maximum(jnp.max(jnp.abs(x), axis=1, keepdims=True), TINY)
                code = jnp.round(x * (LEVELS / largest)).astype(jnp.int32).astype(jnp.int16)
                stat = jnp.where(row_lane == 2 * heads + h + j, largest * (1.0 / LEVELS), stat)
                first = (h + j - c * span) * home
                for d in range(insts):
                    p_send[d, c, first : first + home, :] = code[d * home : (d + 1) * home]
        high, low = split(sums)
        stat = stat + dot(owner_t2, jnp.concatenate([high, low], axis=0))
        for d in range(insts):
            s_send[d, c] = stat[d * home : (d + 1) * home]
        for o in ORDER:
            to = lax.rem(me + o, insts)
            for copies, src, dst, ssem, rsem in (
                (s_copies, s_send, s_recv, s_ssem, s_rsem),
                (p_copies, p_send, p_recv, p_ssem, p_rsem),
            ):
                copy = pltpu.make_async_remote_copy(
                    src_ref=src.at[to, c],
                    dst_ref=dst.at[o - 1, c],
                    send_sem=ssem.at[c, o - 1],
                    recv_sem=rsem.at[c, o - 1],
                    device_id={"inst": to},
                    device_id_type=MESH,
                )
                copy.start()
                copies.append(copy)

    lower = iota((8, 128), 0) < part
    r_copies = []
    half = span * part
    others = insts - 1
    for c in range(CHUNKS):
        for copy in s_copies[c * others : (c + 1) * others]:
            copy.wait_recv()
        stats = [s_send[me, c]] + [s_recv[o, c] for o in range(others)]
        highest = own
        for s in stats:
            highest = jnp.maximum(highest, s)
        own_factor = jnp.exp(own - highest)
        total = own_factor
        factors = []
        for s in stats:
            f = jnp.exp(s - highest)
            total = total + f * pltpu.roll(s, 128 - heads, 1)
            factors.append(f * pltpu.roll(s, 128 - 2 * heads, 1))
        inverse = 1.0 / total
        own_factor = own_factor * inverse
        factors = [f * inverse for f in factors]
        for copy in p_copies[c * others : (c + 1) * others]:
            copy.wait_recv()
        merged = []
        for h in range(c * span, (c + 1) * span):
            at = slice((h - c * span) * home, (h + 1 - c * span) * home)
            acc = own_factor[:, h : h + 1] * own_v
            acc = acc + factors[0][:, h : h + 1] * p_send[me, c, at, :].astype(F32)
            for o in range(others):
                acc = acc + factors[o + 1][:, h : h + 1] * p_recv[o, c, at, :].astype(F32)
            merged.append(acc)
        for u in range(home // 8):
            first, second = [], []
            for h in range(0, span, 2):
                a = merged[h][u * 8 : (u + 1) * 8]
                b = merged[h + 1][u * 8 : (u + 1) * 8]
                first.append(jnp.where(lower, a, pltpu.roll(b, part, 0)))
                second.append(jnp.where(lower, pltpu.roll(a, part, 0), b))
            r_send[2 * u, c] = jnp.concatenate(first, axis=0).astype(BF16)
            r_send[2 * u + 1, c] = jnp.concatenate(second, axis=0).astype(BF16)
        for t in range(tps):
            copy = pltpu.make_async_remote_copy(
                src_ref=r_send.at[t, c],
                dst_ref=out_ref.at[tp, pl.ds(c * half, half)],
                send_sem=r_ssem.at[c, t],
                recv_sem=r_rsem.at[c, tp],
                device_id={"section": after, "tp": t},
                device_id_type=MESH,
            )
            copy.start()
            r_copies.append(copy)
    for c in range(CHUNKS):
        for t in range(tps):
            pltpu.make_async_remote_copy(
                src_ref=r_send.at[t, c],
                dst_ref=out_ref.at[t, pl.ds(c * half, half)],
                send_sem=r_ssem.at[c, t],
                recv_sem=r_rsem.at[c, t],
                device_id={"section": after, "tp": t},
                device_id_type=MESH,
            ).wait_recv()
    for copy in q_copies + s_copies + p_copies + r_copies:
        copy.wait_send()


def shards(queries, new_kv, kv_pages, lengths, block_tables):
    sections = lax.axis_size("section")
    insts = lax.axis_size("inst")
    tps = lax.axis_size("tp")
    home = queries.shape[1]
    heads = queries.shape[2] // HEAD_DIM
    pool, page = kv_pages.shape[1], kv_pages.shape[3]
    rows, slots = block_tables.shape[1:]
    part = home // tps
    sizes = (sections, insts, tps, home, pool, slots, page, heads)
    others = insts - 1
    groups, stack, wide = pool // GROUP, heads * GROUP, heads // CHUNKS * home
    out = pl.pallas_call(
        functools.partial(kernel, sizes),
        out_shape=pltpu.VMEM((tps, heads * part, HEAD_DIM), BF16),
        in_specs=[pl.BlockSpec(memory_space=pltpu.HBM)] * 5,
        out_specs=pl.BlockSpec(memory_space=pltpu.VMEM),
        scratch_shapes=[
            pltpu.VMEM((rows, heads * HEAD_DIM), BF16),
            pltpu.VMEM((2 * home, HEAD_DIM), BF16),
            pltpu.VMEM((2 * home, HEAD_DIM), F32),
            pltpu.VMEM((pool, 2, page, HEAD_DIM), BF16),
            pltpu.VMEM((1, rows), jnp.int32),
            pltpu.VMEM((slots, 1, rows), jnp.int32),
            pltpu.VMEM((groups, stack, 128), F32),
            pltpu.VMEM((groups, stack, 128), F32),
            pltpu.VMEM((heads, pool, HEAD_DIM), F32),
            pltpu.VMEM((heads, pool, HEAD_DIM), F32),
            pltpu.VMEM((heads, pool, HEAD_DIM), F32),
            pltpu.VMEM((insts, CHUNKS, wide, HEAD_DIM), jnp.int16),
            pltpu.VMEM((others, CHUNKS, wide, HEAD_DIM), jnp.int16),
            pltpu.VMEM((insts, CHUNKS, home, 128), F32),
            pltpu.VMEM((others, CHUNKS, home, 128), F32),
            pltpu.VMEM((tps, CHUNKS, heads // CHUNKS * part, HEAD_DIM), BF16),
            pltpu.SemaphoreType.DMA((4,)),
            pltpu.SemaphoreType.DMA((4,)),
            pltpu.SemaphoreType.DMA((others,)),
            pltpu.SemaphoreType.DMA((others,)),
            pltpu.SemaphoreType.DMA((CHUNKS, others)),
            pltpu.SemaphoreType.DMA((CHUNKS, others)),
            pltpu.SemaphoreType.DMA((CHUNKS, others)),
            pltpu.SemaphoreType.DMA((CHUNKS, others)),
            pltpu.SemaphoreType.DMA((CHUNKS, tps)),
            pltpu.SemaphoreType.DMA((CHUNKS, tps)),
        ],
        compiler_params=pltpu.CompilerParams(
            collective_id=0, has_side_effects=True, vmem_limit_bytes=32 * 1024 * 1024
        ),
    )(
        *(
            pltpu.with_memory_space_constraint(x, pltpu.HBM)
            for x in (
                queries[0],
                new_kv[0].reshape(2 * home, HEAD_DIM),
                kv_pages[0],
                lengths,
                jnp.transpose(block_tables, (2, 0, 1)),
            )
        )
    )
    out = out.reshape(tps, heads, part, HEAD_DIM).transpose(2, 0, 1, 3)
    return out.reshape(1, part, tps * heads * HEAD_DIM)


def solution(mesh):
    placed = (
        P("section", "inst", "tp"),
        P("section", "inst", None, "tp"),
        P("section", "inst", None, None, "tp"),
        P("section", None),
        P("section", None, None),
    )
    return jax.shard_map(
        shards,
        mesh=mesh,
        in_specs=placed,
        out_specs=P("section", ("inst", "tp"), None),
        check_vma=False,
    )
```

time: 43.1 us -> 32.8 us (0.76)
  Pallas kernels: 37.1 us -> 32 us
  local copies, waits for them, and re-layouts: 5.72 us -> 0.63 us
    pallas_call x1, Pallas kernels: 37.1 us -> 32 us  [shards(): pl.pallas_call(functools.partial(kernel, sizes), out_shape=pltpu.VMEM((tp...]
    unnamed x10 -> x1, local copies, waits for them, and re-layouts: 5.72 us -> 0.63 us
where the time goes in v2:
time: 32.8 us; the launch traced here: 32.7 us
  Pallas kernels  32 us (98%)
  local copies, waits for them, and re-layouts  0.63 us (2%)
    pallas_call x1, Pallas kernels, shards(): pl.pallas_call(functools.partial(kernel, sizes), out_shape=pltpu.VMEM((tp...  32 us

profile of v2, /device:TPU:1, one launch (start us, length us, event | category | flops | bytes accessed | tf_op | source)
XLA Modules:
  0.0 32.7 jit_solution(13113740917635055711)
XLA Ops:
  0.0 32.0 %shard_map.55 = bf16[8,32,128]{2,1,0:T(8,128)(2,1)S(1)} custom-call(bf16[32,1024]{1,0:T(8,128)(2,1)} %bitcast.11, bf16[64,128]{1,0:T(8,128)(2,1)} %bitcast.12, bf16[128,2,64,128]{3,2,1,0:T(8,128)(2,1)} %bitcast.10, s32[1,128]{1,0:T(1,128)} %len_hbm.1, s32[7,1,128]{2,1,0:T(1,128)} %bitcast.13), custom_call_target="tpu_custom_call" | custom-call | tf_op jit(solution)/shard_map/pallas_call | solution.py:328
  32.0 0.6 %copy.8 = bf16[1,4,8192]{2,1,0:T(4,128)(2,1)} copy(bf16[1,4,8192]{2,1,0:T(4,128)(2,1)S(1)} %bitcast.9) | data formatting | bytes 131072

commit v3 on v2

v3 whole, which is shorter than its diff:
```python
import functools
import math

import jax
import jax.numpy as jnp
from jax import lax
from jax.experimental import pallas as pl
from jax.experimental.pallas import tpu as pltpu
from jax.sharding import PartitionSpec as P

HEAD_DIM = 128
NEGATIVE = -1e30
GROUP = 8
CHUNKS = 2
ORDER = (1, 3, 2)
LEVELS = 32767.0
TINY = 1e-30
MESH = pl.DeviceIdType.MESH
F32 = jnp.float32
BF16 = jnp.bfloat16


def iota(shape, dim):
    return lax.broadcasted_iota(jnp.int32, shape, dim)


def dot(a, b):
    return lax.dot_general(a, b, (((1,), (0,)), ((), ())), preferred_element_type=F32)


def dot_nt(a, b):
    return lax.dot_general(a, b, (((1,), (1,)), ((), ())), preferred_element_type=F32)


def split(x):
    high = x.astype(BF16)
    return high, (x - high.astype(F32)).astype(BF16)


def arrived(ref, sem):
    pltpu.make_async_copy(ref, ref, sem).wait()


def kernel(
    sizes,
    q_hbm,
    fresh_hbm,
    kv_hbm,
    len_hbm,
    table_hbm,
    out_ref,
    q_all,
    fresh,
    fresh_f,
    kv,
    length,
    table,
    score_buf,
    weight_buf,
    page_x,
    page_m,
    page_s,
    p_send,
    p_recv,
    s_send,
    s_recv,
    r_send,
    load_sem,
    kv_sem,
    q_ssem,
    q_rsem,
    p_ssem,
    p_rsem,
    s_ssem,
    s_rsem,
    r_ssem,
    r_rsem,
):
    sections, insts, tps, home, pool, slots, page, heads = sizes
    rows = home * insts
    part = home // tps
    scale = 1.0 / math.sqrt(HEAD_DIM)
    sec = lax.axis_index("section")
    me = lax.axis_index("inst")
    tp = lax.axis_index("tp")
    before = lax.rem(sec + sections - 1, sections)
    after = lax.rem(sec + 1, sections)
    my_rows = pl.ds(pl.multiple_of(me * home, home), home)

    span = heads // CHUNKS
    width = span * HEAD_DIM
    load_q = [
        pltpu.make_async_copy(
            q_hbm.at[:, pl.ds(c * width, width)], q_all.at[c, my_rows], load_sem.at[c]
        )
        for c in range(CHUNKS)
    ]
    for copy in load_q:
        copy.start()

    barrier = pltpu.get_barrier_semaphore()
    for o in range(1, insts):
        pl.semaphore_signal(
            barrier, inc=1, device_id={"inst": lax.rem(me + o, insts)}, device_id_type=MESH
        )
    for t in range(tps):
        pl.semaphore_signal(
            barrier, inc=1, device_id={"section": before, "tp": t}, device_id_type=MESH
        )
    load_fresh = pltpu.make_async_copy(fresh_hbm, fresh, load_sem.at[CHUNKS])
    load_len = pltpu.make_async_copy(len_hbm, length, load_sem.at[CHUNKS + 1])
    load_table = pltpu.make_async_copy(table_hbm, table, load_sem.at[CHUNKS + 2])
    parts = kv_sem.shape[0]
    per = pool // parts
    load_kv = [
        pltpu.make_async_copy(
            kv_hbm.at[pl.ds(c * per, per)], kv.at[pl.ds(c * per, per)], kv_sem.at[c]
        )
        for c in range(parts)
    ]
    for copy in [load_table, load_len, load_fresh] + load_kv:
        copy.start()
    pl.semaphore_wait(barrier, insts - 1 + tps)

    for c in range(CHUNKS):
        load_q[c].wait()
        for o in ORDER:
            copy = pltpu.make_async_remote_copy(
                src_ref=q_all.at[c, my_rows],
                dst_ref=q_all.at[c, my_rows],
                send_sem=q_ssem.at[c],
                recv_sem=q_rsem.at[c],
                device_id={"inst": lax.rem(me + o, insts)},
                device_id_type=MESH,
            )
            copy.start()

    load_len.wait()
    load_table.wait()
    page_id = iota((pool, rows), 0)
    counted = jnp.zeros((pool, rows), jnp.int32)
    for k in range(slots):
        local = table[k] - me * pool
        live = jnp.clip(length[...] - k * page, 0, page)
        counted = counted + jnp.where(page_id == local, live, 0)
    owned = counted > 0
    owner_f = jnp.where(owned, 1.0, 0.0).astype(F32)
    owner = owner_f.astype(BF16)
    owner_t = owner_f.T.astype(BF16)
    owner_t2 = jnp.concatenate([owner_t, owner_t], axis=1)
    tokens = dot(counted.astype(F32).astype(BF16), jnp.ones((rows, 128), BF16))

    load_fresh.wait()
    fresh_f[...] = fresh[...].astype(F32)
    own_k = fresh_f[pl.ds(0, home, stride=2), :]
    own_v = fresh_f[pl.ds(1, home, stride=2), :]
    lane = iota((home, 128), 1)
    own = jnp.zeros((home, 128), F32)
    for c in range(CHUNKS):
        q_mine = q_all[c, my_rows, :].astype(F32)
        for h in range(span):
            score = jnp.sum(q_mine[:, h * 128 : (h + 1) * 128] * own_k, axis=1, keepdims=True)
            own = jnp.where(lane == c * span + h, score * scale, own)

    for copy in load_kv:
        copy.wait()

    others = insts - 1
    stack = span * GROUP
    groups = pool // GROUP
    row_page = lax.rem(iota((stack, 128), 0), GROUP)
    per_tile = 128 // page
    tiles = GROUP // per_tile
    tile_of = row_page // per_tile
    token = iota((stack, 128), 1) - lax.rem(row_page, per_tile) * page
    token_f = token.astype(F32)
    pool_lane = iota((pool, 128), 1)
    row_lane = iota((rows, 128), 1)
    for c in range(CHUNKS):
        arrived(q_all.at[c, pl.ds(0, others * home)], q_rsem.at[c])
        picked = dot(owner, q_all[c])
        for g in range(groups):
            at = slice(g * GROUP, (g + 1) * GROUP)
            group_q = jnp.concatenate(
                [picked[at, h * 128 : (h + 1) * 128] for h in range(span)], axis=0
            ).astype(BF16)
            full = dot_nt(group_q, kv[at, 0].reshape(GROUP * page, 128))
            scores = full[:, :128]
            for i in range(1, tiles):
                scores = jnp.where(tile_of == i, full[:, i * 128 : (i + 1) * 128], scores)
            score_buf[c, g] = scores
        for g in range(groups):
            at = slice(g * GROUP, (g + 1) * GROUP)
            limit = jnp.concatenate([tokens[at]] * span, axis=0)
            valid = (token >= 0) & (token_f < limit)
            scores = jnp.where(valid, score_buf[c, g] * scale, NEGATIVE)
            highest = jnp.max(scores, axis=1, keepdims=True)
            weights = jnp.where(valid, jnp.exp(scores - highest), 0.0)
            total = jnp.sum(weights, axis=1, keepdims=True)
            weight_buf[c, g] = weights
            page_m[c, :, at, :] = jnp.broadcast_to(highest, (stack, 128)).reshape(span, GROUP, 128)
            page_s[c, :, at, :] = jnp.broadcast_to(total, (stack, 128)).reshape(span, GROUP, 128)
        for g in range(groups):
            at = slice(g * GROUP, (g + 1) * GROUP)
            weights = weight_buf[c, g]
            spread = jnp.concatenate(
                [jnp.where(tile_of == i, weights, 0.0).astype(BF16) for i in range(tiles)], axis=1
            )
            x = dot(spread, kv[at, 1].reshape(GROUP * page, 128))
            page_x[c, :, at, :] = x.reshape(span, GROUP, 128)

        refs = []
        for h in range(span):
            rounded = page_m[c, h].astype(BF16).astype(F32)
            refs.append(jnp.max(jnp.where(owned, rounded, NEGATIVE), axis=0, keepdims=True))
        sums = jnp.zeros((pool, 128), F32)
        stat = jnp.concatenate(refs + [jnp.zeros((128 - span, rows), F32)], axis=0).T
        for h in range(0, span, 2):
            sides = []
            for j in (h, h + 1):
                page_ref = dot_nt(owner, jnp.broadcast_to(refs[j], (128, rows)).astype(BF16))
                factor = jnp.exp(page_m[c, j] - page_ref)
                sums = jnp.where(pool_lane == span + j, factor * page_s[c, j], sums)
                high, low = split(factor * page_x[c, j])
                sides.append(jnp.concatenate([high, low], axis=0))
            both = dot(owner_t2, jnp.concatenate(sides, axis=1))
            for j in range(2):
                x = both[:, j * 128 : (j + 1) * 128]
                largest = jnp.maximum(jnp.max(jnp.abs(x), axis=1, keepdims=True), TINY)
                code = jnp.round(x * (LEVELS / largest)).astype(jnp.int32).astype(jnp.int16)
                stat = jnp.where(row_lane == 2 * span + h + j, largest * (1.0 / LEVELS), stat)
                first = (h + j) * home
                for d in range(insts):
                    p_send[d, c, first : first + home, :] = code[d * home : (d + 1) * home]
        high, low = split(sums)
        stat = stat + dot(owner_t2, jnp.concatenate([high, low], axis=0))
        for d in range(insts):
            s_send[d, c] = stat[d * home : (d + 1) * home]
        for o in ORDER:
            to = lax.rem(me + o, insts)
            for src, dst, ssem, rsem in (
                (s_send, s_recv, s_ssem, s_rsem),
                (p_send, p_recv, p_ssem, p_rsem),
            ):
                copy = pltpu.make_async_remote_copy(
                    src_ref=src.at[to, c],
                    dst_ref=dst.at[c, o - 1],
                    send_sem=ssem.at[c],
                    recv_sem=rsem.at[c],
                    device_id={"inst": to},
                    device_id_type=MESH,
                )
                copy.start()

    lower = iota((8, 128), 0) < part
    half = span * part
    for c in range(CHUNKS):
        arrived(s_recv.at[c], s_rsem.at[c])
        stats = [s_send[me, c]] + [s_recv[c, o] for o in range(others)]
        mine = pltpu.roll(own, 128 - c * span, 1) if c else own
        highest = mine
        for s in stats:
            highest = jnp.maximum(highest, s)
        own_factor = jnp.exp(mine - highest)
        total = own_factor
        factors = []
        for s in stats:
            f = jnp.exp(s - highest)
            total = total + f * pltpu.roll(s, 128 - span, 1)
            factors.append(f * pltpu.roll(s, 128 - 2 * span, 1))
        inverse = 1.0 / total
        own_factor = own_factor * inverse
        factors = [f * inverse for f in factors]
        arrived(p_recv.at[c], p_rsem.at[c])
        merged = []
        for h in range(span):
            at = slice(h * home, (h + 1) * home)
            acc = own_factor[:, h : h + 1] * own_v
            acc = acc + factors[0][:, h : h + 1] * p_send[me, c, at, :].astype(F32)
            for o in range(others):
                acc = acc + factors[o + 1][:, h : h + 1] * p_recv[c, o, at, :].astype(F32)
            merged.append(acc)
        for u in range(home // 8):
            first, second = [], []
            for h in range(0, span, 2):
                a = merged[h][u * 8 : (u + 1) * 8]
                b = merged[h + 1][u * 8 : (u + 1) * 8]
                first.append(jnp.where(lower, a, pltpu.roll(b, part, 0)))
                second.append(jnp.where(lower, pltpu.roll(a, part, 0), b))
            r_send[c, 2 * u] = jnp.concatenate(first, axis=0).astype(BF16)
            r_send[c, 2 * u + 1] = jnp.concatenate(second, axis=0).astype(BF16)
        for t in range(tps):
            copy = pltpu.make_async_remote_copy(
                src_ref=r_send.at[c, t],
                dst_ref=out_ref.at[tp, pl.ds(c * half, half)],
                send_sem=r_ssem.at[c],
                recv_sem=r_rsem.at[c],
                device_id={"section": after, "tp": t},
                device_id_type=MESH,
            )
            copy.start()
    for c in range(CHUNKS):
        arrived(q_all.at[c, pl.ds(0, others * home)], q_ssem.at[c])
        arrived(s_recv.at[c], s_ssem.at[c])
        arrived(p_recv.at[c], p_ssem.at[c])
        arrived(r_send.at[c], r_ssem.at[c])
    for c in range(CHUNKS):
        arrived(r_send.at[c], r_rsem.at[c])


def shards(queries, new_kv, kv_pages, lengths, block_tables):
    sections = lax.axis_size("section")
    insts = lax.axis_size("inst")
    tps = lax.axis_size("tp")
    home = queries.shape[1]
    heads = queries.shape[2] // HEAD_DIM
    pool, page = kv_pages.shape[1], kv_pages.shape[3]
    rows, slots = block_tables.shape[1:]
    part = home // tps
    sizes = (sections, insts, tps, home, pool, slots, page, heads)
    others = insts - 1
    span = heads // CHUNKS
    groups, stack, wide = pool // GROUP, span * GROUP, span * home
    out = pl.pallas_call(
        functools.partial(kernel, sizes),
        out_shape=pltpu.VMEM((tps, heads * part, HEAD_DIM), BF16),
        in_specs=[pl.BlockSpec(memory_space=pltpu.HBM)] * 5,
        out_specs=pl.BlockSpec(memory_space=pltpu.VMEM),
        scratch_shapes=[
            pltpu.VMEM((CHUNKS, rows, span * HEAD_DIM), BF16),
            pltpu.VMEM((2 * home, HEAD_DIM), BF16),
            pltpu.VMEM((2 * home, HEAD_DIM), F32),
            pltpu.VMEM((pool, 2, page, HEAD_DIM), BF16),
            pltpu.VMEM((1, rows), jnp.int32),
            pltpu.VMEM((slots, 1, rows), jnp.int32),
            pltpu.VMEM((CHUNKS, groups, stack, 128), F32),
            pltpu.VMEM((CHUNKS, groups, stack, 128), F32),
            pltpu.VMEM((CHUNKS, span, pool, HEAD_DIM), F32),
            pltpu.VMEM((CHUNKS, span, pool, HEAD_DIM), F32),
            pltpu.VMEM((CHUNKS, span, pool, HEAD_DIM), F32),
            pltpu.VMEM((insts, CHUNKS, wide, HEAD_DIM), jnp.int16),
            pltpu.VMEM((CHUNKS, others, wide, HEAD_DIM), jnp.int16),
            pltpu.VMEM((insts, CHUNKS, home, 128), F32),
            pltpu.VMEM((CHUNKS, others, home, 128), F32),
            pltpu.VMEM((CHUNKS, tps, span * part, HEAD_DIM), BF16),
            pltpu.SemaphoreType.DMA((CHUNKS + 3,)),
            pltpu.SemaphoreType.DMA((4,)),
            pltpu.SemaphoreType.DMA((CHUNKS,)),
            pltpu.SemaphoreType.DMA((CHUNKS,)),
            pltpu.SemaphoreType.DMA((CHUNKS,)),
            pltpu.SemaphoreType.DMA((CHUNKS,)),
            pltpu.SemaphoreType.DMA((CHUNKS,)),
            pltpu.SemaphoreType.DMA((CHUNKS,)),
            pltpu.SemaphoreType.DMA((CHUNKS,)),
            pltpu.SemaphoreType.DMA((CHUNKS,)),
        ],
        compiler_params=pltpu.CompilerParams(
            collective_id=0, has_side_effects=True, vmem_limit_bytes=32 * 1024 * 1024
        ),
    )(
        *(
            pltpu.with_memory_space_constraint(x, pltpu.HBM)
            for x in (
                queries[0],
                new_kv[0].reshape(2 * home, HEAD_DIM),
                kv_pages[0],
                lengths,
                jnp.transpose(block_tables, (2, 0, 1)),
            )
        )
    )
    out = out.reshape(tps, heads, part, HEAD_DIM).transpose(2, 0, 1, 3)
    return out.reshape(1, part, tps * heads * HEAD_DIM)


def solution(mesh):
    placed = (
        P("section", "inst", "tp"),
        P("section", "inst", None, "tp"),
        P("section", "inst", None, None, "tp"),
        P("section", None),
        P("section", None, None),
    )
    return jax.shard_map(
        shards,
        mesh=mesh,
        in_specs=placed,
        out_specs=P("section", ("inst", "tp"), None),
        check_vma=False,
    )
```

time: 32.8 us -> 31.8 us (0.970)
  Pallas kernels: 32 us -> 31.1 us
    pallas_call x1, Pallas kernels: 32 us -> 31.1 us  [shards(): pl.pallas_call(functools.partial(kernel, sizes), out_shape=pltpu.VMEM((tp...]
where the time goes in v3:
time: 31.8 us; the launch traced here: 31.7 us
  Pallas kernels  31.1 us (98%)
  local copies, waits for them, and re-layouts  0.63 us (2%)
    pallas_call x1, Pallas kernels, shards(): pl.pallas_call(functools.partial(kernel, sizes), out_shape=pltpu.VMEM((tp...  31.1 us

profile of v3, /device:TPU:1, one launch (start us, length us, event | category | flops | bytes accessed | tf_op | source)
XLA Modules:
  0.0 31.7 jit_solution(6093738637214966511)
XLA Ops:
  0.0 31.1 %shard_map.55 = bf16[8,32,128]{2,1,0:T(8,128)(2,1)S(1)} custom-call(bf16[32,1024]{1,0:T(8,128)(2,1)} %bitcast.11, bf16[64,128]{1,0:T(8,128)(2,1)} %bitcast.12, bf16[128,2,64,128]{3,2,1,0:T(8,128)(2,1)} %bitcast.10, s32[1,128]{1,0:T(1,128)} %len_hbm.1, s32[7,1,128]{2,1,0:T(1,128)} %bitcast.13), custom_call_target="tpu_custom_call" | custom-call | tf_op jit(solution)/shard_map/pallas_call | solution.py:324
  31.1 0.6 %copy.8 = bf16[1,4,8192]{2,1,0:T(4,128)(2,1)} copy(bf16[1,4,8192]{2,1,0:T(4,128)(2,1)S(1)} %bitcast.9) | data formatting | bytes 131072

commit v4 on v3

--- a/solution.py
+++ b/solution.py
@@ -53,8 +53,11 @@
     fresh,
     fresh_f,
     kv,
+    keys,
     length,
     table,
+    picked_buf,
+    token_buf,
     score_buf,
     weight_buf,
     page_x,
@@ -148,7 +151,7 @@
     owner = owner_f.astype(BF16)
     owner_t = owner_f.T.astype(BF16)
     owner_t2 = jnp.concatenate([owner_t, owner_t], axis=1)
-    tokens = dot(counted.astype(F32).astype(BF16), jnp.ones((rows, 128), BF16))
+    token_buf[...] = dot(counted.astype(F32).astype(BF16), jnp.ones((rows, 128), BF16))
 
     load_fresh.wait()
     fresh_f[...] = fresh[...].astype(F32)
@@ -162,8 +165,11 @@
             score = jnp.sum(q_mine[:, h * 128 : (h + 1) * 128] * own_k, axis=1, keepdims=True)
             own = jnp.where(lane == c * span + h, score * scale, own)
 
-    for copy in load_kv:
-        copy.wait()
+    for i in range(parts):
+        load_kv[i].wait()
+        for g in range(i * per // GROUP, (i + 1) * per // GROUP):
+            at = slice(g * GROUP, (g + 1) * GROUP)
+            keys[g] = kv[at, 0].reshape(GROUP * page, 128).T
 
     others = insts - 1
     stack = span * GROUP
@@ -176,39 +182,51 @@
     token_f = token.astype(F32)
     pool_lane = iota((pool, 128), 1)
     row_lane = iota((rows, 128), 1)
-    for c in range(CHUNKS):
+    def wait_q(c):
         arrived(q_all.at[c, pl.ds(0, others * home)], q_rsem.at[c])
-        picked = dot(owner, q_all[c])
-        for g in range(groups):
-            at = slice(g * GROUP, (g + 1) * GROUP)
-            group_q = jnp.concatenate(
-                [picked[at, h * 128 : (h + 1) * 128] for h in range(span)], axis=0
-            ).astype(BF16)
-            full = dot_nt(group_q, kv[at, 0].reshape(GROUP * page, 128))
-            scores = full[:, :128]
-            for i in range(1, tiles):
-                scores = jnp.where(tile_of == i, full[:, i * 128 : (i + 1) * 128], scores)
-            score_buf[c, g] = scores
-        for g in range(groups):
-            at = slice(g * GROUP, (g + 1) * GROUP)
-            limit = jnp.concatenate([tokens[at]] * span, axis=0)
-            valid = (token >= 0) & (token_f < limit)
-            scores = jnp.where(valid, score_buf[c, g] * scale, NEGATIVE)
-            highest = jnp.max(scores, axis=1, keepdims=True)
-            weights = jnp.where(valid, jnp.exp(scores - highest), 0.0)
-            total = jnp.sum(weights, axis=1, keepdims=True)
-            weight_buf[c, g] = weights
-            page_m[c, :, at, :] = jnp.broadcast_to(highest, (stack, 128)).reshape(span, GROUP, 128)
-            page_s[c, :, at, :] = jnp.broadcast_to(total, (stack, 128)).reshape(span, GROUP, 128)
-        for g in range(groups):
-            at = slice(g * GROUP, (g + 1) * GROUP)
-            weights = weight_buf[c, g]
-            spread = jnp.concatenate(
-                [jnp.where(tile_of == i, weights, 0.0).astype(BF16) for i in range(tiles)], axis=1
-            )
-            x = dot(spread, kv[at, 1].reshape(GROUP * page, 128))
-            page_x[c, :, at, :] = x.reshape(span, GROUP, 128)
-
+
+    def pick(c):
+        picked_buf[c] = dot(owner, q_all[c])
+
+    def score_group(c, g, carry):
+        at = pl.ds(pl.multiple_of(g * GROUP, GROUP), GROUP)
+        group_q = jnp.concatenate(
+            [picked_buf[c, at, h * 128 : (h + 1) * 128] for h in range(span)], axis=0
+        ).astype(BF16)
+        full = dot(group_q, keys[g])
+        scores = full[:, :128]
+        for i in range(1, tiles):
+            scores = jnp.where(tile_of == i, full[:, i * 128 : (i + 1) * 128], scores)
+        score_buf[c, g] = scores
+        return carry
+
+    def weigh_group(c, g, carry):
+        at = pl.ds(pl.multiple_of(g * GROUP, GROUP), GROUP)
+        limit = jnp.concatenate([token_buf[at, :]] * span, axis=0)
+        valid = (token >= 0) & (token_f < limit)
+        scores = jnp.where(valid, score_buf[c, g] * scale, NEGATIVE)
+        highest = jnp.max(scores, axis=1, keepdims=True)
+        weights = jnp.where(valid, jnp.exp(scores - highest), 0.0)
+        total = jnp.sum(weights, axis=1, keepdims=True)
+        weight_buf[c, g] = weights
+        page_m[c, :, at, :] = jnp.broadcast_to(highest, (stack, 128)).reshape(span, GROUP, 128)
+        page_s[c, :, at, :] = jnp.broadcast_to(total, (stack, 128)).reshape(span, GROUP, 128)
+        return carry
+
+    def value_group(c, g, carry):
+        at = pl.ds(pl.multiple_of(g * GROUP, GROUP), GROUP)
+        weights = weight_buf[c, g]
+        spread = jnp.concatenate(
+            [jnp.where(tile_of == i, weights, 0.0).astype(BF16) for i in range(tiles)], axis=1
+        )
+        x = dot(spread, kv[at, 1].reshape(GROUP * page, 128))
+        page_x[c, :, at, :] = x.reshape(span, GROUP, 128)
+        return carry
+
+    def groupwise(body, c):
+        lax.fori_loop(0, groups, functools.partial(body, c), 0, unroll=groups)
+
+    def combine(c):
         refs = []
         for h in range(span):
             rounded = page_m[c, h].astype(BF16).astype(F32)
@@ -236,6 +254,8 @@
         stat = stat + dot(owner_t2, jnp.concatenate([high, low], axis=0))
         for d in range(insts):
             s_send[d, c] = stat[d * home : (d + 1) * home]
+
+    def send(c):
         for o in ORDER:
             to = lax.rem(me + o, insts)
             for src, dst, ssem, rsem in (
@@ -251,6 +271,21 @@
                     device_id_type=MESH,
                 )
                 copy.start()
+
+    wait_q(0)
+    pick(0)
+    groupwise(score_group, 0)
+    groupwise(weigh_group, 0)
+    groupwise(value_group, 0)
+    combine(0)
+    send(0)
+    wait_q(1)
+    pick(1)
+    groupwise(score_group, 1)
+    groupwise(weigh_group, 1)
+    groupwise(value_group, 1)
+    combine(1)
+    send(1)
 
     lower = iota((8, 128), 0) < part
     half = span * part
@@ -331,8 +366,11 @@
             pltpu.VMEM((2 * home, HEAD_DIM), BF16),
             pltpu.VMEM((2 * home, HEAD_DIM), F32),
             pltpu.VMEM((pool, 2, page, HEAD_DIM), BF16),
+            pltpu.VMEM((groups, HEAD_DIM, GROUP * page), BF16),
             pltpu.VMEM((1, rows), jnp.int32),
             pltpu.VMEM((slots, 1, rows), jnp.int32),
+            pltpu.VMEM((CHUNKS, pool, span * HEAD_DIM), F32),
+            pltpu.VMEM((pool, 128), F32),
             pltpu.VMEM((CHUNKS, groups, stack, 128), F32),
             pltpu.VMEM((CHUNKS, groups, stack, 128), F32),
             pltpu.VMEM((CHUNKS, span, pool, HEAD_DIM), F32),

time: 31.8 us -> 31 us (0.975)
  Pallas kernels: 31.1 us -> 30.2 us
    pallas_call x1, Pallas kernels: 31.1 us -> 30.2 us  [shards(): pl.pallas_call(functools.partial(kernel, sizes), out_shape=pltpu.VMEM((tp...]
where the time goes in v4:
time: 31 us; the launch traced here: 30.8 us
  Pallas kernels  30.2 us (97%)
  local copies, waits for them, and re-layouts  0.63 us (2%)
    pallas_call x1, Pallas kernels, shards(): pl.pallas_call(functools.partial(kernel, sizes), out_shape=pltpu.VMEM((tp...  30.2 us
    unnamed x1, local copies, waits for them, and re-layouts  0.63 us

profile of v4, /device:TPU:1, one launch (start us, length us, event | category | flops | bytes accessed | tf_op | source)
XLA Modules:
  0.0 30.8 jit_solution(13636662638829666848)
XLA Ops:
  0.0 30.2 %shard_map.55 = bf16[8,32,128]{2,1,0:T(8,128)(2,1)S(1)} custom-call(bf16[32,1024]{1,0:T(8,128)(2,1)} %bitcast.11, bf16[64,128]{1,0:T(8,128)(2,1)} %bitcast.12, bf16[128,2,64,128]{3,2,1,0:T(8,128)(2,1)} %bitcast.10, s32[1,128]{1,0:T(1,128)} %len_hbm.1, s32[7,1,128]{2,1,0:T(1,128)} %bitcast.13), custom_call_target="tpu_custom_call" | custom-call | tf_op jit(solution)/shard_map/pallas_call | solution.py:359
  30.2 0.6 %copy.8 = bf16[1,4,8192]{2,1,0:T(4,128)(2,1)} copy(bf16[1,4,8192]{2,1,0:T(4,128)(2,1)S(1)} %bitcast.9) | data formatting | bytes 131072

commit v5 on v4

--- a/solution.py
+++ b/solution.py
@@ -68,6 +68,8 @@
     s_send,
     s_recv,
     r_send,
+    own_send,
+    own_recv,
     load_sem,
     kv_sem,
     q_ssem,
@@ -78,6 +80,7 @@
     s_rsem,
     r_ssem,
     r_rsem,
+    own_sem,
 ):
     sections, insts, tps, home, pool, slots, page, heads = sizes
     rows = home * insts
@@ -86,6 +89,10 @@
     sec = lax.axis_index("section")
     me = lax.axis_index("inst")
     tp = lax.axis_index("tp")
+    core = lax.rem(tp, 2)
+    merger = tp + 1 - core
+    merges = core == 1
+    others = insts - 1
     before = lax.rem(sec + sections - 1, sections)
     after = lax.rem(sec + 1, sections)
     my_rows = pl.ds(pl.multiple_of(me * home, home), home)
@@ -106,10 +113,21 @@
         pl.semaphore_signal(
             barrier, inc=1, device_id={"inst": lax.rem(me + o, insts)}, device_id_type=MESH
         )
-    for t in range(tps):
+    for t in range(1, tps, 2):
         pl.semaphore_signal(
             barrier, inc=1, device_id={"section": before, "tp": t}, device_id_type=MESH
         )
+
+    @pl.when(merges)
+    def _():
+        for o in range(insts):
+            pl.semaphore_signal(
+                barrier,
+                inc=1,
+                device_id={"inst": lax.rem(me + o, insts), "tp": tp - 1},
+                device_id_type=MESH,
+            )
+
     load_fresh = pltpu.make_async_copy(fresh_hbm, fresh, load_sem.at[CHUNKS])
     load_len = pltpu.make_async_copy(len_hbm, length, load_sem.at[CHUNKS + 1])
     load_table = pltpu.make_async_copy(table_hbm, table, load_sem.at[CHUNKS + 2])
@@ -123,7 +141,15 @@
     ]
     for copy in [load_table, load_len, load_fresh] + load_kv:
         copy.start()
-    pl.semaphore_wait(barrier, insts - 1 + tps)
+
+    @pl.when(merges)
+    def _():
+        pl.semaphore_wait(barrier, others + tps)
+
+    @pl.when(jnp.logical_not(merges))
+    def _():
+        pl.semaphore_wait(barrier, others + insts)
+
 
     for c in range(CHUNKS):
         load_q[c].wait()
@@ -165,13 +191,26 @@
             score = jnp.sum(q_mine[:, h * 128 : (h + 1) * 128] * own_k, axis=1, keepdims=True)
             own = jnp.where(lane == c * span + h, score * scale, own)
 
+    own_send[0] = own
+    own_send[1] = own_v
+
+    @pl.when(jnp.logical_not(merges))
+    def _():
+        pltpu.make_async_remote_copy(
+            src_ref=own_send,
+            dst_ref=own_recv,
+            send_sem=own_sem.at[0],
+            recv_sem=own_sem.at[1],
+            device_id={"tp": merger},
+            device_id_type=MESH,
+        ).start()
+
     for i in range(parts):
         load_kv[i].wait()
         for g in range(i * per // GROUP, (i + 1) * per // GROUP):
             at = slice(g * GROUP, (g + 1) * GROUP)
             keys[g] = kv[at, 0].reshape(GROUP * page, 128).T
 
-    others = insts - 1
     stack = span * GROUP
     groups = pool // GROUP
     row_page = lax.rem(iota((stack, 128), 0), GROUP)
@@ -256,21 +295,27 @@
             s_send[d, c] = stat[d * home : (d + 1) * home]
 
     def send(c):
-        for o in ORDER:
+        def send_to(o, slot):
             to = lax.rem(me + o, insts)
             for src, dst, ssem, rsem in (
                 (s_send, s_recv, s_ssem, s_rsem),
                 (p_send, p_recv, p_ssem, p_rsem),
             ):
-                copy = pltpu.make_async_remote_copy(
+                pltpu.make_async_remote_copy(
                     src_ref=src.at[to, c],
-                    dst_ref=dst.at[c, o - 1],
+                    dst_ref=dst.at[c, slot],
                     send_sem=ssem.at[c],
-                    recv_sem=rsem.at[c],
-                    device_id={"inst": to},
+                    recv_sem=rsem.at[c, core],
+                    device_id={"inst": to, "tp": merger},
                     device_id_type=MESH,
-                )
-                copy.start()
+                ).start()
+
+        for o in ORDER:
+            send_to(o, o - 1 + core * others)
+
+        @pl.when(jnp.logical_not(merges))
+        def _():
+            send_to(0, 2 * others)
 
     wait_q(0)
     pick(0)
@@ -289,9 +334,8 @@
 
     lower = iota((8, 128), 0) < part
     half = span * part
-    for c in range(CHUNKS):
-        arrived(s_recv.at[c], s_rsem.at[c])
-        stats = [s_send[me, c]] + [s_recv[c, o] for o in range(others)]
+
+    def merge(c, k, own, own_v, stats, codes):
         mine = pltpu.roll(own, 128 - c * span, 1) if c else own
         highest = mine
         for s in stats:
@@ -306,14 +350,12 @@
         inverse = 1.0 / total
         own_factor = own_factor * inverse
         factors = [f * inverse for f in factors]
-        arrived(p_recv.at[c], p_rsem.at[c])
         merged = []
         for h in range(span):
             at = slice(h * home, (h + 1) * home)
             acc = own_factor[:, h : h + 1] * own_v
-            acc = acc + factors[0][:, h : h + 1] * p_send[me, c, at, :].astype(F32)
-            for o in range(others):
-                acc = acc + factors[o + 1][:, h : h + 1] * p_recv[c, o, at, :].astype(F32)
+            for f, code in zip(factors, codes):
+                acc = acc + f[:, h : h + 1] * code(at).astype(F32)
             merged.append(acc)
         for u in range(home // 8):
             first, second = [], []
@@ -322,25 +364,66 @@
                 b = merged[h + 1][u * 8 : (u + 1) * 8]
                 first.append(jnp.where(lower, a, pltpu.roll(b, part, 0)))
                 second.append(jnp.where(lower, pltpu.roll(a, part, 0), b))
-            r_send[c, 2 * u] = jnp.concatenate(first, axis=0).astype(BF16)
-            r_send[c, 2 * u + 1] = jnp.concatenate(second, axis=0).astype(BF16)
+            r_send[c, k, 2 * u] = jnp.concatenate(first, axis=0).astype(BF16)
+            r_send[c, k, 2 * u + 1] = jnp.concatenate(second, axis=0).astype(BF16)
+
+    def send_rows(c, k):
         for t in range(tps):
-            copy = pltpu.make_async_remote_copy(
-                src_ref=r_send.at[c, t],
-                dst_ref=out_ref.at[tp, pl.ds(c * half, half)],
+            pltpu.make_async_remote_copy(
+                src_ref=r_send.at[c, k, t],
+                dst_ref=out_ref.at[tp - 1 + k, pl.ds(c * half, half)],
                 send_sem=r_ssem.at[c],
                 recv_sem=r_rsem.at[c],
                 device_id={"section": after, "tp": t},
                 device_id_type=MESH,
+            ).start()
+
+    @pl.when(merges)
+    def _():
+        for c in range(CHUNKS):
+            received = [lambda at, c=c, o=o: p_recv[c, o, at, :] for o in range(2 * others + 1)]
+            near = [o for o in range(others)] + [2 * others]
+            far = [o + others for o in range(others)]
+            arrived(s_recv.at[c, pl.ds(0, others)], s_rsem.at[c, 1])
+            arrived(p_recv.at[c, pl.ds(0, others)], p_rsem.at[c, 1])
+            merge(
+                c,
+                1,
+                own_send[0],
+                own_send[1],
+                [s_send[me, c]] + [s_recv[c, o] for o in far],
+                [lambda at, c=c: p_send[me, c, at, :]] + [received[o] for o in far],
             )
-            copy.start()
+            send_rows(c, 1)
+            if c == 0:
+                arrived(own_recv, own_sem.at[1])
+            arrived(s_recv.at[c, pl.ds(0, insts)], s_rsem.at[c, 0])
+            arrived(p_recv.at[c, pl.ds(0, insts)], p_rsem.at[c, 0])
+            merge(
+                c,
+                0,
+                own_recv[0],
+                own_recv[1],
+                [s_recv[c, o] for o in near],
+                [received[o] for o in near],
+            )
+            send_rows(c, 0)
+        for c in range(CHUNKS):
+            arrived(s_recv.at[c, pl.ds(0, others)], s_ssem.at[c])
+            arrived(p_recv.at[c, pl.ds(0, others)], p_ssem.at[c])
+            arrived(r_send.at[c], r_ssem.at[c])
+
+    @pl.when(jnp.logical_not(merges))
+    def _():
+        arrived(own_send, own_sem.at[0])
+        for c in range(CHUNKS):
+            arrived(s_recv.at[c, pl.ds(0, insts)], s_ssem.at[c])
+            arrived(p_recv.at[c, pl.ds(0, insts)], p_ssem.at[c])
+
     for c in range(CHUNKS):
         arrived(q_all.at[c, pl.ds(0, others * home)], q_ssem.at[c])
-        arrived(s_recv.at[c], s_ssem.at[c])
-        arrived(p_recv.at[c], p_ssem.at[c])
-        arrived(r_send.at[c], r_ssem.at[c])
     for c in range(CHUNKS):
-        arrived(r_send.at[c], r_rsem.at[c])
+        arrived(r_send.at[c, 0], r_rsem.at[c])
 
 
 def shards(queries, new_kv, kv_pages, lengths, block_tables):
@@ -377,20 +460,23 @@
             pltpu.VMEM((CHUNKS, span, pool, HEAD_DIM), F32),
             pltpu.VMEM((CHUNKS, span, pool, HEAD_DIM), F32),
             pltpu.VMEM((insts, CHUNKS, wide, HEAD_DIM), jnp.int16),
-            pltpu.VMEM((CHUNKS, others, wide, HEAD_DIM), jnp.int16),
+            pltpu.VMEM((CHUNKS, 2 * others + 1, wide, HEAD_DIM), jnp.int16),
             pltpu.VMEM((insts, CHUNKS, home, 128), F32),
-            pltpu.VMEM((CHUNKS, others, home, 128), F32),
-            pltpu.VMEM((CHUNKS, tps, span * part, HEAD_DIM), BF16),
+            pltpu.VMEM((CHUNKS, 2 * others + 1, home, 128), F32),
+            pltpu.VMEM((CHUNKS, 2, tps, span * part, HEAD_DIM), BF16),
+            pltpu.VMEM((2, home, 128), F32),
+            pltpu.VMEM((2, home, 128), F32),
             pltpu.SemaphoreType.DMA((CHUNKS + 3,)),
             pltpu.SemaphoreType.DMA((4,)),
             pltpu.SemaphoreType.DMA((CHUNKS,)),
             pltpu.SemaphoreType.DMA((CHUNKS,)),
             pltpu.SemaphoreType.DMA((CHUNKS,)),
+            pltpu.SemaphoreType.DMA((CHUNKS, 2)),
+            pltpu.SemaphoreType.DMA((CHUNKS,)),
+            pltpu.SemaphoreType.DMA((CHUNKS, 2)),
             pltpu.SemaphoreType.DMA((CHUNKS,)),
             pltpu.SemaphoreType.DMA((CHUNKS,)),
-            pltpu.SemaphoreType.DMA((CHUNKS,)),
-            pltpu.SemaphoreType.DMA((CHUNKS,)),
-            pltpu.SemaphoreType.DMA((CHUNKS,)),
+            pltpu.SemaphoreType.DMA((2,)),
         ],
         compiler_params=pltpu.CompilerParams(
             collective_id=0, has_side_effects=True, vmem_limit_bytes=32 * 1024 * 1024

time: 31 us -> 30.6 us (0.987)
    pallas_call x1, Pallas kernels: 30.2 us -> 29.9 us  [shards(): pl.pallas_call(functools.partial(kernel, sizes), out_shape=pltpu.VMEM((tp...]
where the time goes in v5:
time: 30.6 us; the launch traced here: 30.5 us
  Pallas kernels  29.9 us (98%)
  local copies, waits for them, and re-layouts  0.63 us (2%)
    pallas_call x1, Pallas kernels, shards(): pl.pallas_call(functools.partial(kernel, sizes), out_shape=pltpu.VMEM((tp...  29.9 us
    unnamed x1, local copies, waits for them, and re-layouts  0.63 us

profile of v5, /device:TPU:1, one launch (start us, length us, event | category | flops | bytes accessed | tf_op | source)
XLA Modules:
  0.0 30.5 jit_solution(6421593813851772527)
XLA Ops:
  0.0 29.9 %shard_map.55 = bf16[8,32,128]{2,1,0:T(8,128)(2,1)S(1)} custom-call(bf16[32,1024]{1,0:T(8,128)(2,1)} %bitcast.11, bf16[64,128]{1,0:T(8,128)(2,1)} %bitcast.12, bf16[128,2,64,128]{3,2,1,0:T(8,128)(2,1)} %bitcast.10, s32[1,128]{1,0:T(1,128)} %len_hbm.1, s32[7,1,128]{2,1,0:T(1,128)} %bitcast.13), custom_call_target="tpu_custom_call" | custom-call | tf_op jit(solution)/shard_map/pallas_call | solution.py:442
  29.9 0.6 %copy.8 = bf16[1,4,8192]{2,1,0:T(4,128)(2,1)} copy(bf16[1,4,8192]{2,1,0:T(4,128)(2,1)S(1)} %bitcast.9) | data formatting | bytes 131072

commit v6 on v5

--- a/solution.py
+++ b/solution.py
@@ -12,7 +12,7 @@
 NEGATIVE = -1e30
 GROUP = 8
 CHUNKS = 2
-ORDER = (1, 3, 2)
+ORDER = (2, 1, 3)
 LEVELS = 32767.0
 TINY = 1e-30
 MESH = pl.DeviceIdType.MESH
@@ -265,6 +265,13 @@
     def groupwise(body, c):
         lax.fori_loop(0, groups, functools.partial(body, c), 0, unroll=groups)
 
+    lanes = 128 // (home // 8)
+
+    def unpack(block):
+        return jnp.concatenate(
+            [block] + [pltpu.roll(block, 128 - i * lanes, 1) for i in range(1, home // 8)], axis=0
+        )
+
     def combine(c):
         refs = []
         for h in range(span):
@@ -292,7 +299,11 @@
         high, low = split(sums)
         stat = stat + dot(owner_t2, jnp.concatenate([high, low], axis=0))
         for d in range(insts):
-            s_send[d, c] = stat[d * home : (d + 1) * home]
+            block = stat[d * home : d * home + 8]
+            for i in range(1, home // 8):
+                first = d * home + 8 * i
+                block = block + pltpu.roll(stat[first : first + 8], i * lanes, 1)
+            s_send[d, c] = block
 
     def send(c):
         def send_to(o, slot):
@@ -391,7 +402,7 @@
                 1,
                 own_send[0],
                 own_send[1],
-                [s_send[me, c]] + [s_recv[c, o] for o in far],
+                [unpack(s_send[me, c])] + [unpack(s_recv[c, o]) for o in far],
                 [lambda at, c=c: p_send[me, c, at, :]] + [received[o] for o in far],
             )
             send_rows(c, 1)
@@ -404,7 +415,7 @@
                 0,
                 own_recv[0],
                 own_recv[1],
-                [s_recv[c, o] for o in near],
+                [unpack(s_recv[c, o]) for o in near],
                 [received[o] for o in near],
             )
             send_rows(c, 0)
@@ -461,8 +472,8 @@
             pltpu.VMEM((CHUNKS, span, pool, HEAD_DIM), F32),
             pltpu.VMEM((insts, CHUNKS, wide, HEAD_DIM), jnp.int16),
             pltpu.VMEM((CHUNKS, 2 * others + 1, wide, HEAD_DIM), jnp.int16),
-            pltpu.VMEM((insts, CHUNKS, home, 128), F32),
-            pltpu.VMEM((CHUNKS, 2 * others + 1, home, 128), F32),
+            pltpu.VMEM((insts, CHUNKS, 8, 128), F32),
+            pltpu.VMEM((CHUNKS, 2 * others + 1, 8, 128), F32),
             pltpu.VMEM((CHUNKS, 2, tps, span * part, HEAD_DIM), BF16),
             pltpu.VMEM((2, home, 128), F32),
             pltpu.VMEM((2, home, 128), F32),

time: 30.6 us -> 30.1 us (0.984)
  Pallas kernels: 29.9 us -> 29.4 us
    pallas_call x1, Pallas kernels: 29.9 us -> 29.4 us  [shards(): pl.pallas_call(functools.partial(kernel, sizes), out_shape=pltpu.VMEM((tp...]
where the time goes in v6:
time: 30.1 us; the launch traced here: 30 us
  Pallas kernels  29.4 us (98%)
  local copies, waits for them, and re-layouts  0.63 us (2%)
    pallas_call x1, Pallas kernels, shards(): pl.pallas_call(functools.partial(kernel, sizes), out_shape=pltpu.VMEM((tp...  29.4 us
    unnamed x1, local copies, waits for them, and re-layouts  0.63 us

profile of v6, /device:TPU:1, one launch (start us, length us, event | category | flops | bytes accessed | tf_op | source)
XLA Modules:
  0.0 30.0 jit_solution(4089443009824784213)
XLA Ops:
  0.0 29.4 %shard_map.55 = bf16[8,32,128]{2,1,0:T(8,128)(2,1)S(1)} custom-call(bf16[32,1024]{1,0:T(8,128)(2,1)} %bitcast.11, bf16[64,128]{1,0:T(8,128)(2,1)} %bitcast.12, bf16[128,2,64,128]{3,2,1,0:T(8,128)(2,1)} %bitcast.10, s32[1,128]{1,0:T(1,128)} %len_hbm.1, s32[7,1,128]{2,1,0:T(1,128)} %bitcast.13), custom_call_target="tpu_custom_call" | custom-call | tf_op jit(solution)/shard_map/pallas_call | solution.py:453
  29.4 0.6 %copy.8 = bf16[1,4,8192]{2,1,0:T(4,128)(2,1)} copy(bf16[1,4,8192]{2,1,0:T(4,128)(2,1)S(1)} %bitcast.9) | data formatting | bytes 131072
